TPU v7x, 32 devices: a whole 2x2x4 slice. The times are simulated.
32 devices in a mesh: lat: 4 (over z), lon: 4 (over y, x), mem: 2 (over core).
Axes of the slice: x: 2, y: 2, z: 4, core: 2. Of those that a mesh axis runs over, the one named last changes fastest.
Arguments:
- measured_inputs: bfloat16 [512, 128, 256], P(('lat', 'lon', 'mem')), may hold values from -6 to 6
- target_sector: int32 [512], P(('lat', 'lon', 'mem')), may hold values from 0 to 3, as said below
- hidden_member_fields: bfloat16 [2, 32, 32, 768], P('mem', 'lat', 'lon'), may hold values from -6 to 6
- analysis_adjoint: bfloat16 [2, 32, 32, 768], P('mem', 'lat', 'lon'), may hold values from -0.29882812 to 0.29882812
- inner_perceptron_coeffs: bfloat16 [256, 256], replicated, may hold values from -0.375 to 0.375
- outer_perceptron_coeffs: bfloat16 [256, 768], replicated, may hold values from -0.375 to 0.375
- probe_projector: bfloat16 [768, 768], replicated, may hold values from -0.21875 to 0.21875
- logit_sharpness: float32 [12], replicated, may hold values from 0.5 to 2.5
- adjacent_channel_coeffs: float32 [8, 768], replicated, may hold values from -0.7 to 0.7
Outputs:
- analysis: bfloat16 [2, 32, 32, 768], P('mem', 'lat', 'lon')
- in_weight_grad: float32 [256, 256], replicated
- out_weight_grad: float32 [256, 768], replicated
Inputs may be any that keep to these rules, and one draw needn't show every extreme that they name: `target_sector`: of the 16 blocks of one device at most 8 have one destination, and one destination has exactly 8; in every band and member one sector receives exactly 8 blocks from every device of the band, 32 in all, and no sector receives more.
All inputs are finite; a program needn't handle non-finite values.
Results may differ from a plain program's by a relative error of at most 0.012.
The roundings to bfloat16 on the way count: a program that leaves them out, or rounds other values in their place, can miss the bound.
Values may be sent and summed in bfloat16 or wider, within the bound.
A program may use at most 192 MiB of HBM per device.

v0:
```python
import math

import jax
import jax.numpy as jnp
from jax import lax
from jax.sharding import PartitionSpec as P

HEADS = 12
CHANNELS_PER_ATT = 64


NEIGHBOURS = ((-1, -1), (-1, 0), (-1, 1), (0, -1), (0, 1), (1, -1), (1, 0), (1, 1))


def extended(block, sides, width):
    for axis, dim in sides:
        count = lax.axis_size(axis)
        forward = [(i, i + 1) for i in range(count - 1)]
        forward.append((count - 1, 0))
        backward = [(target, source) for source, target in forward]
        low = lax.ppermute(
            lax.slice_in_dim(block, block.shape[dim] - width, None, axis=dim), axis, forward
        )
        high = lax.ppermute(lax.slice_in_dim(block, 0, width, axis=dim), axis, backward)
        block = jnp.concatenate([low, block, high], axis=dim)
    return block


def silu_slope(pre_act):
    sigmoid_val = jax.nn.sigmoid(pre_act)
    return sigmoid_val * (1.0 + pre_act * (1.0 - sigmoid_val))


def mix_local(padded, keep_rows, adjacent_channel_coeffs, direction):
    values = padded.astype(jnp.float32) * keep_rows[:, None, None]
    n_rows = padded.shape[0] - 2
    n_cols = padded.shape[1] - 2
    total = values[1 : 1 + n_rows, 1 : 1 + n_cols]
    for offset_idx, (row_step, col_step) in enumerate(NEIGHBOURS):
        row_start = 1 + direction * row_step
        col_start = 1 + direction * col_step
        total = (
            total
            + adjacent_channel_coeffs[offset_idx]
            * values[row_start : row_start + n_rows, col_start : col_start + n_cols]
        )
    return total


def mutual_attention_apply(
    probe_projection,
    grid_point_entries,
    lookup_projection_entries,
    genuine_entry_indicator,
    logit_sharpness,
):
    n_cells = grid_point_entries.shape[0]
    n_tokens = lookup_projection_entries.shape[0]
    query_heads = probe_projection.reshape(n_cells, HEADS, CHANNELS_PER_ATT)
    key_heads = lookup_projection_entries.reshape(n_tokens, HEADS, CHANNELS_PER_ATT)
    latent_heads = grid_point_entries.reshape(n_cells, HEADS, CHANNELS_PER_ATT)
    normaliser_entries = logit_sharpness / math.sqrt(CHANNELS_PER_ATT)
    scores = jnp.einsum("qhd,khd->hqk", query_heads, key_heads, preferred_element_type=jnp.float32)
    scores = jnp.where(
        genuine_entry_indicator[None, None, :], scores * normaliser_entries[:, None, None], -jnp.inf
    )
    self_score = jnp.einsum(
        "qhd,qhd->hq", query_heads, latent_heads, preferred_element_type=jnp.float32
    )
    self_score = self_score * normaliser_entries[:, None]
    row_max = jnp.maximum(jnp.max(scores, axis=2), self_score)
    exp_terms = jnp.exp(scores - row_max[:, :, None])
    self_exp = jnp.exp(self_score - row_max)
    denominator = jnp.sum(exp_terms, axis=2) + self_exp
    probs = exp_terms / denominator[:, :, None]
    self_prob = self_exp / denominator
    weights = probs.astype(jnp.bfloat16)
    self_weight = lax.optimization_barrier(self_prob.astype(jnp.bfloat16)).astype(jnp.float32)
    update = jnp.einsum("hqk,khd->qhd", weights, key_heads, preferred_element_type=jnp.float32)
    update = update + jnp.transpose(self_weight)[:, :, None] * latent_heads.astype(jnp.float32)
    revised_analysis = (
        grid_point_entries.astype(jnp.float32) + update.reshape(n_cells, HEADS * CHANNELS_PER_ATT)
    ).astype(jnp.bfloat16)
    return (revised_analysis, (probs, self_prob, weights))


def mutual_attention_adjoint(
    probe_projection,
    grid_point_entries,
    lookup_projection_entries,
    retained_intermediates,
    hidden_field_adjoint,
    logit_sharpness,
):
    probs, self_prob, weights = retained_intermediates
    n_cells = grid_point_entries.shape[0]
    n_tokens = lookup_projection_entries.shape[0]
    query_heads = probe_projection.reshape(n_cells, HEADS, CHANNELS_PER_ATT)
    key_heads = lookup_projection_entries.reshape(n_tokens, HEADS, CHANNELS_PER_ATT)
    latent_heads = grid_point_entries.reshape(n_cells, HEADS, CHANNELS_PER_ATT)
    grad_heads = hidden_field_adjoint.reshape(n_cells, HEADS, CHANNELS_PER_ATT)
    normaliser_entries = logit_sharpness / math.sqrt(CHANNELS_PER_ATT)
    weight_grad = jnp.einsum(
        "qhd,khd->hqk", grad_heads, key_heads, preferred_element_type=jnp.float32
    )
    self_grad = jnp.einsum(
        "qhd,qhd->hq", grad_heads, latent_heads, preferred_element_type=jnp.float32
    )
    row_total = jnp.sum(probs * weight_grad, axis=2) + self_prob * self_grad
    logit_grad = (
        probs * (weight_grad - row_total[:, :, None]) * normaliser_entries[:, None, None]
    ).astype(jnp.bfloat16)
    measured_embedding_adjoint = jnp.einsum(
        "hqk,qhd->khd", weights, grad_heads, preferred_element_type=jnp.float32
    )
    measured_embedding_adjoint = measured_embedding_adjoint + jnp.einsum(
        "hqk,qhd->khd", logit_grad, query_heads, preferred_element_type=jnp.float32
    )
    return measured_embedding_adjoint.reshape(n_tokens, HEADS * CHANNELS_PER_ATT).astype(
        jnp.bfloat16
    )


def per_device(
    measured_inputs,
    target_sector,
    hidden_member_fields,
    analysis_adjoint,
    inner_perceptron_coeffs,
    outer_perceptron_coeffs,
    probe_projector,
    logit_sharpness,
    adjacent_channel_coeffs,
):
    lon_count = lax.axis_size("lon")
    lat_count = lax.axis_size("lat")
    block_count = target_sector.shape[0]
    block_len = measured_inputs.shape[1]
    obs_width = measured_inputs.shape[2]
    model_width = hidden_member_fields.shape[3]
    hidden_width = inner_perceptron_coeffs.shape[1]
    cell_rows = hidden_member_fields.shape[1]
    cell_cols = hidden_member_fields.shape[2]
    n_cells = cell_rows * cell_cols
    cap_slots = max(2, 2 * block_count // lon_count)
    sector_ids = jnp.arange(lon_count, dtype=jnp.int32)
    one_hot = (target_sector[:, None] == sector_ids[None, :]).astype(jnp.int32)
    earlier = jnp.cumsum(one_hot, axis=0) - one_hot
    slot_index = target_sector * cap_slots + jnp.sum(earlier * one_hot, axis=1)
    cot_padded = extended(analysis_adjoint[0], (("lat", 0), ("lon", 1)), 1)
    band_targets = lax.all_gather(target_sector, "lon", axis=0, tiled=True)
    own_sector = lax.axis_index("lon")
    arrivals = jnp.sum(
        (band_targets == own_sector).astype(jnp.int32).reshape(lon_count, block_count), axis=1
    )
    live_slots = jnp.arange(cap_slots, dtype=jnp.int32)[None, :] < arrivals[:, None]
    genuine_entry_indicator = jnp.broadcast_to(
        live_slots[:, :, None], (lon_count, cap_slots, block_len)
    ).reshape(-1)
    grid_point_entries = hidden_member_fields.reshape(n_cells, model_width)
    probe_projection = jnp.dot(
        grid_point_entries, probe_projector, preferred_element_type=jnp.float32
    ).astype(jnp.bfloat16)
    send_blocks = jnp.zeros((lon_count * cap_slots, block_len, obs_width), jnp.bfloat16)
    send_blocks = (
        send_blocks.at[slot_index]
        .set(measured_inputs)
        .reshape(lon_count, cap_slots, block_len, obs_width)
    )
    obs_blocks = lax.all_to_all(send_blocks, "lon", split_axis=0, concat_axis=0, tiled=True)
    pre_act = jnp.dot(obs_blocks, inner_perceptron_coeffs, preferred_element_type=jnp.float32)
    hidden_act = jax.nn.silu(pre_act).astype(jnp.bfloat16)
    obs_feat = jnp.dot(
        hidden_act, outer_perceptron_coeffs, preferred_element_type=jnp.float32
    ).astype(jnp.bfloat16)
    token_blocks, pre_act, hidden_act, obs_feat = (obs_blocks, pre_act, hidden_act, obs_feat)
    lookup_projection_entries = obs_feat.reshape(-1, model_width)
    revised_analysis, retained_intermediates = mutual_attention_apply(
        probe_projection,
        grid_point_entries,
        lookup_projection_entries,
        genuine_entry_indicator,
        logit_sharpness,
    )
    state_grid = revised_analysis.reshape(cell_rows, cell_cols, model_width)
    state_padded = extended(state_grid, (("lat", 0), ("lon", 1)), 1)
    lat_index = lax.axis_index("lat")
    keep_rows = jnp.ones((cell_rows + 2,), jnp.float32)
    keep_rows = keep_rows.at[0].set(jnp.where(lat_index > 0, 1.0, 0.0))
    keep_rows = keep_rows.at[cell_rows + 1].set(jnp.where(lat_index < lat_count - 1, 1.0, 0.0))
    analysis = (
        mix_local(state_padded, keep_rows, adjacent_channel_coeffs, 1)
        .astype(jnp.bfloat16)
        .reshape(hidden_member_fields.shape)
    )
    hidden_field_adjoint = (
        mix_local(cot_padded, keep_rows, adjacent_channel_coeffs, -1)
        .astype(jnp.bfloat16)
        .reshape(n_cells, model_width)
    )
    measured_embedding_adjoint = mutual_attention_adjoint(
        probe_projection,
        grid_point_entries,
        lookup_projection_entries,
        retained_intermediates,
        hidden_field_adjoint,
        logit_sharpness,
    )
    grad_blocks = measured_embedding_adjoint.reshape(lon_count, cap_slots, block_len, model_width)
    grad_rows = grad_blocks.reshape(-1, model_width)
    hidden_rows = hidden_act.reshape(-1, hidden_width)
    pre_rows = pre_act.reshape(-1, hidden_width)
    hidden_grad = jnp.einsum(
        "td,hd->th", grad_rows, outer_perceptron_coeffs, preferred_element_type=jnp.float32
    )
    hidden_grad = (hidden_grad * silu_slope(pre_rows)).astype(jnp.bfloat16)
    out_grad = jnp.einsum("th,td->hd", hidden_rows, grad_rows, preferred_element_type=jnp.float32)
    in_grad = jnp.einsum(
        "tc,th->ch",
        token_blocks.reshape(-1, obs_width),
        hidden_grad,
        preferred_element_type=jnp.float32,
    )
    in_grad, out_grad = lax.psum((in_grad, out_grad), ("lat", "lon", "mem"))
    return (analysis, in_grad, out_grad)


def solution(mesh):
    in_specs = (
        P(("lat", "lon", "mem"), None, None),
        P(("lat", "lon", "mem")),
        P("mem", "lat", "lon", None),
        P("mem", "lat", "lon", None),
        P(),
        P(),
        P(),
        P(),
        P(),
    )
    out_specs = (P("mem", "lat", "lon", None), P(), P())
    return jax.shard_map(
        per_device, mesh=mesh, in_specs=in_specs, out_specs=out_specs, check_vma=False
    )
```

profile of v0, /device:TPU:0, one launch (start us, length us, event | category | flops | bytes accessed | tf_op | source)
XLA Modules:
  0.0 304.1 jit_solution(4965517322944199355)
XLA Ops:
  9.6 1.6 broadcast_in_dim.20
  11.2 3.4 %scatter_fusion = bf16[32,128,256]{2,1,0:T(8,128)(2,1)} fusion(bf16[32,128,256]{2,1,0:T(8,128)(2,1)} %broadcast_in_dim.20, s32[16]{0:T(128)S(1)} %compare_select_fusion, bf16[16,128,256]{2,1,0:T(8,128)(2,1)} %param.13), kind=kCustom, calls=%fused_computation | custom fusion | bytes 3145792 | tf_op jit(solution)/shard_map/scatter | solution.py:167
  14.6 5.2 %all-to-all-start = ((bf16[4,8,128,256]{3,2,1,0:T(8,128)(2,1)}), bf16[4,8,128,256]{3,2,1,0:T(8,128)(2,1)S(1)}, u32[]{:S(2)}, u32[]{:S(2)}) async-start(bf16[4,8,128,256]{3,2,1,0:T(8,128)(2,1)} %bitcast.5), calls=%async_computation | async-start | bytes 4194304 | tf_op jit(solution)/shard_map/all_to_all | solution.py:170
  19.8 3.6 %collective-permute-start.5 = (bf16[1,8,768]{2,1,0:T(8,128)(2,1)S(1)}, bf16[1,8,768]{2,1,0:T(8,128)(2,1)S(1)}, u32[]{:S(2)}, u32[]{:S(2)}) collective-permute-start(bf16[1,8,768]{2,1,0:T(8,128)(2,1)S(1)} %get-tuple-element.48), channel_id=1, source_target_pairs={{8,0},{16,8},{24,16},{0,24},{9,1},{17,9},{25,17},{1,25},{10,2},{18... | collective-permute-start | bytes 36872 | tf_op jit(solution)/shard_map/ppermute | solution.py:24
  24.9 22.9 %all-reduce.1 = s32[64]{0:T(128)S(1)} all-reduce(s32[64]{0:T(128)S(1)} %dynamic-update-slice.6), channel_id=1, replica_groups=mesh['lat'=4,'lon'=4,'mem'=2] {'lon'}, use_global_device_ids=true, to_apply=%add.1 | all-reduce | flops 64 | bytes 512
  48.2 1.0 convolution_convert_fusion.1
  49.6 1.7 collective-permute-start.6
  51.3 1.1 slice_reduce_fusion.7
  53.5 1.1 reshape.144
  56.8 4.3 %multiply_convert_fusion.2 = (bf16[4,8,128,256]{3,2,1,0:T(8,128)(2,1)S(1)}, f32[4,8,128,256]{3,2,1,0:T(8,128)}) fusion(bf16[4,8,128,256]{3,2,1,0:T(8,128)(2,1)S(1)} %all-to-all-done, bf16[256,256]{1,0:T(8,128)(2,1)} %param.17), kind=kOutput, calls=%fused_computation.20 | convolution fusion | flops 542113792 | bytes 8519680 | tf_op jit(solution)/shard_map/dot_general | solution.py:171
  61.1 1.4 copy-done.4
  62.4 4.5 %convolution_convert_fusion = bf16[4,8,128,768]{3,2,1,0:T(8,128)(2,1)} fusion(bf16[4,8,128,256]{3,2,1,0:T(8,128)(2,1)S(1)} %get-tuple-element.49, bf16[256,768]{1,0:T(8,128)(2,1)S(1)} %copy-done.5), kind=kOutput, calls=%fused_computation.21 | convolution fusion | flops 1613758464 | bytes 8781824 | tf_op jit(solution)/shard_map/dot_general | solution.py:173
  66.9 9.0 %copy.22 = bf16[4,8,128,768]{2,1,0,3:T(8,128)(2,1)} copy(bf16[4,8,128,768]{3,2,1,0:T(8,128)(2,1)} %convolution_convert_fusion) | data formatting | bytes 12582912 | tf_op jit(solution)/shard_map/convert_element_type | solution.py:175
  75.9 10.4 %reshape_reshape.11 = bf16[4096,12,64]{0,2,1:T(8,128)(2,1)} reshape(bf16[4,8,128,768]{2,1,0,3:T(8,128)(2,1)} %copy.22) | data formatting | bytes 12582912 | tf_op jit(solution)/shard_map/reshape;reshape | solution.py:60
  86.2 4.1 %fusion = (f32[12,64]{1,0:T(8,128)S(1)}, f32[12,64,4096]{2,1,0:T(8,128)S(1)}) fusion(f32[12]{0:T(128)S(1)} %broadcast_multiply_fusion, pred[4096]{0:T(1024)(128)(4,1)S(1)} %broadcast_bitcast_fusion, bf16[64,12,64]{0,2,1:T(8,128)(2,1)S(1)} %copy-done.7, bf16[4096,12,64]{0,2,1:T(8,128)(2,1)} %reshape_reshape.11), kind=kOutput, calls=%fused_computation.6 | convolution fusion | flops 412089600 | bytes 18979888 | tf_op jit(solution)/shard_map/qhd,khd->hqk/dot_general | solution.py:63
  90.5 3.1 %fusion.2 = f32[12,64]{1,0:T(8,128)S(1)} fusion(f32[12,64,4096]{2,1,0:T(8,128)S(1)} %get-tuple-element.52, f32[12,64]{1,0:T(8,128)S(1)} %multiply_maximum_fusion, f32[12]{0:T(128)S(1)} %broadcast_multiply_fusion, pred[4096]{0:T(1024)(128)(4,1)S(1)} %broadcast_bitcast_fusion), kind=kLoop, calls=%fused_computation.8 | loop fusion | flops 12582144 | bytes 12593200 | tf_op jit(solution)/shard_map/reduce_sum | solution.py:74
  93.7 4.1 %copy-done.3 = bf16[4096,12,64]{0,2,1:T(8,128)(2,1)S(1)} copy-done((bf16[4096,12,64]{0,2,1:T(8,128)(2,1)S(1)}, bf16[4096,12,64]{0,2,1:T(8,128)(2,1)}, u32[]{:S(2)}) %copy-start.3) | copy-done | bytes 6291480
  97.7 7.3 %multiply_reduce_fusion = (f32[12,64]{1,0:T(8,128)S(1)}, f32[12,64,4096]{2,1,0:T(8,128)}) fusion(f32[12,64]{1,0:T(8,128)S(1)} %fusion.53, f32[12,64]{1,0:T(8,128)S(1)} %multiply_maximum_fusion, f32[12,64,4096]{2,1,0:T(8,128)S(1)} %get-tuple-element.52, f32[12]{0:T(128)S(1)} %broadcast_multiply_fusion, pred[4096]{0:T(1024)(128)(4,1)S(1)} %broadcast_bitcast_fusion, ...), kind=kOutput, calls=%fused_computation.3 | convolution fusion | flops 421526784 | bytes 31568944 | tf_op jit(solution)/shard_map/qhd,khd->hqk/dot_general | solution.py:103
  105.0 6.7 %fusion.11 = f32[12,64,4096]{2,1,0:T(8,128)} fusion(bf16[64,12,64]{2,1,0:T(8,128)(2,1)S(1)} %copy-done.9, f32[12,64,4096]{2,1,0:T(8,128)S(1)} %get-tuple-element.52, f32[12,64]{1,0:T(8,128)S(1)} %fusion.53, f32[12,64]{1,0:T(8,128)S(1)} %multiply_maximum_fusion, f32[12]{0:T(128)S(1)} %broadcast_multiply_fusion, pred[4096]{0:T(1024)(128)(4,1)S(1)} %broadcast_bitcast_fusion), kind=kOutput, calls=%fused_computation.22 | convolution fusion | flops 418381824 | bytes 25274416 | tf_op jit(solution)/shard_map/hqk,qhd->khd/dot_general | solution.py:113
  111.9 6.4 %fusion.18 = f32[64,12,64]{0,2,1:T(8,128)S(1)} fusion(bf16[4096,12,64]{0,2,1:T(8,128)(2,1)} %reshape_reshape.11, bf16[64,12,64]{0,2,1:T(8,128)(2,1)S(1)} %copy-done.11, f32[64,12]{0,1:T(8,128)S(1)} %convert_bitcast_fusion, f32[12,64,4096]{2,1,0:T(8,128)S(1)} %get-tuple-element.52, f32[12,64]{1,0:T(8,128)S(1)} %fusion.53, ...), kind=kOutput, calls=%fused_computation.27 | convolution fusion | flops 418529280 | bytes 19182640 | tf_op jit(solution)/shard_map/hqk,khd->qhd/dot_general | solution.py:79
  119.3 0.9 add_convert_fusion.1
  120.3 3.9 %collective-permute-start.1 = (bf16[1,8,768]{2,1,0:T(8,128)(2,1)S(1)}, bf16[1,8,768]{2,1,0:T(8,128)(2,1)S(1)}, u32[]{:S(2)}, u32[]{:S(2)}) collective-permute-start(bf16[1,8,768]{2,1,0:T(8,128)(2,1)S(1)} %get-tuple-element.46), channel_id=1, source_target_pairs={{8,0},{16,8},{24,16},{0,24},{9,1},{17,9},{25,17},{1,25},{10,2},{18... | collective-permute-start | bytes 36872 | tf_op jit(solution)/shard_map/ppermute | solution.py:24
  125.1 5.5 %fusion.10 = f32[4096,256]{1,0:T(8,128)} fusion(f32[4,8,128,256]{3,2,1,0:T(8,128)} %get-tuple-element.50), kind=kLoop, calls=%fused_computation.19 | loop fusion | flops 7340032 | bytes 8388608 | tf_op jit(solution)/shard_map/mul | solution.py:31
  130.6 17.7 %add_convert_fusion = bf16[12,64,4096]{2,1,0:T(8,128)(2,1)} fusion(f32[12,64,4096]{2,1,0:T(8,128)} %fusion.11, bf16[64,12,64]{0,2,1:T(8,128)(2,1)S(1)} %copy-done.7, f32[12,64,4096]{2,1,0:T(8,128)} %get-tuple-element.54, f32[12,64]{1,0:T(8,128)S(1)} %get-tuple-element.39, f32[12]{0:T(128)S(1)} %broadcast_multiply_fusion, f32[12,64,4096]{2,1,0:T(8,128)} %copy-done.2, ...), kind=kOutput, calls=%fused_computation.1 | convolution fusion | flops 434110464 | bytes 44151856 | tf_op jit(solution)/shard_map/hqk,qhd->khd/dot_general | solution.py:116
  148.3 6.1 %fusion.58 = f32[256,768]{1,0:T(8,128)} fusion(bf16[4096,256]{1,0:T(8,128)(2,1)} %bitcast.93, bf16[4096,768]{0,1:T(8,128)(2,1)} %bitcast.91), kind=kOutput, calls=%fused_computation.114 | convolution fusion | flops 1610612736 | bytes 9175040 | tf_op jit(solution)/shard_map/th,td->hd/dot_general | solution.py:217
  154.4 7.5 %fusion.21 = f32[256,256]{1,0:T(8,128)} fusion(bf16[4096,256]{1,0:T(8,128)(2,1)S(1)} %bitcast.90, f32[4096,256]{1,0:T(8,128)} %fusion.10, bf16[4096,768]{0,1:T(8,128)(2,1)} %bitcast.92, bf16[256,768]{1,0:T(8,128)(2,1)} %param.18), kind=kOutput, calls=%fused_computation.29 | convolution fusion | flops 2149580800 | bytes 13238272 | tf_op jit(solution)/shard_map/tc,th->ch/dot_general | solution.py:218
  163.0 1.2 collective-permute-start.3
  165.1 1.9 collective-permute-done.3
  166.9 2.1 collective-permute-done.2
  169.9 123.6 %all-reduce.5.cloned.1.call-done = (f32[256,256]{1,0:T(8,128)}, f32[256,768]{1,0:T(8,128)}) async-done(((f32[256,256]{1,0:T(8,128)}, f32[256,768]{1,0:T(8,128)}), (f32[256,256]{1,0:T(8,128)}, f32[256,768]{1,0:T(8,128)})) %all-reduce.5.cloned.1.call-update) | async-done | bytes 1048592 | tf_op jit(solution)/shard_map/psum | solution.py:224
  293.5 1.7 copy.59
  295.2 2.1 copy.60
  (79 shorter events, 12.2 us)
Async XLA Ops:
  7.2 41.0 %copy-start = (bf16[768,768]{1,0:T(8,128)(2,1)S(1)}, bf16[768,768]{1,0:T(8,128)(2,1)}, u32[]{:S(2)}) copy-start(bf16[768,768]{1,0:T(8,128)(2,1)} %param.19) | copy-start | bytes 3538948
  7.2 16.3 %copy-start.14 = (u32[32]{0:T(128)S(1)}, u32[32]{0:T(128)}, u32[]{:S(2)}) copy-start(u32[32]{0:T(128)} %constant.92) | copy-start | bytes 388
  7.2 17.5 %copy-start.12 = (s32[16]{0:T(128)S(1)}, s32[16]{0:T(128)}, u32[]{:S(2)}) copy-start(s32[16]{0:T(128)} %param.14) | copy-start | bytes 196
  7.2 12.6 %copy-start.10 = (bf16[1,8,8,768]{3,2,1,0:T(8,128)(2,1)S(1)}, bf16[1,8,8,768]{3,2,1,0:T(8,128)(2,1)}, u32[]{:S(2)}) copy-start(bf16[1,8,8,768]{3,2,1,0:T(8,128)(2,1)} %param.16) | copy-start | bytes 294916
  7.2 41.0 %copy-start.6 = (bf16[1,8,8,768]{3,2,1,0:T(8,128)(2,1)S(1)}, bf16[1,8,8,768]{3,2,1,0:T(8,128)(2,1)}, u32[]{:S(2)}) copy-start(bf16[1,8,8,768]{3,2,1,0:T(8,128)(2,1)} %param.15) | copy-start | bytes 294916
  7.2 41.9 %copy-start.13 = (f32[12]{0:T(128)S(1)}, f32[12]{0:T(128)}, u32[]{:S(2)}) copy-start(f32[12]{0:T(128)} %param.20) | copy-start | bytes 148
  14.6 42.2 %all-to-all-start = ((bf16[4,8,128,256]{3,2,1,0:T(8,128)(2,1)}), bf16[4,8,128,256]{3,2,1,0:T(8,128)(2,1)S(1)}, u32[]{:S(2)}, u32[]{:S(2)}) async-start(bf16[4,8,128,256]{3,2,1,0:T(8,128)(2,1)} %bitcast.5), calls=%async_computation | async-start | bytes 4194304 | tf_op jit(solution)/shard_map/all_to_all | solution.py:170
  19.8 273.7 %all-reduce.5.cloned.1.call-start = ((), (), s32[]{:S(2)}) async-start(), calls=%async_computation.1 | async-start | bytes 2097152 | tf_op jit(solution)/shard_map/psum | solution.py:224
  19.8 29.4 %collective-permute-start.5 = (bf16[1,8,768]{2,1,0:T(8,128)(2,1)S(1)}, bf16[1,8,768]{2,1,0:T(8,128)(2,1)S(1)}, u32[]{:S(2)}, u32[]{:S(2)}) collective-permute-start(bf16[1,8,768]{2,1,0:T(8,128)(2,1)S(1)} %get-tuple-element.48), channel_id=1, source_target_pairs={{8,0},{16,8},{24,16},{0,24},{9,1},{17,9},{25,17},{1,25},{10,2},{18... | collective-permute-start | bytes 36872 | tf_op jit(solution)/shard_map/ppermute | solution.py:24
  23.4 25.8 %collective-permute-start.4 = (bf16[1,8,768]{2,1,0:T(8,128)(2,1)S(1)}, bf16[1,8,768]{2,1,0:T(8,128)(2,1)S(1)}, u32[]{:S(2)}, u32[]{:S(2)}) collective-permute-start(bf16[1,8,768]{2,1,0:T(8,128)(2,1)S(1)} %get-tuple-element.47), channel_id=1, source_target_pairs={{0,8},{8,16},{16,24},{24,0},{1,9},{9,17},{17,25},{25,1},{2,10},{10... | collective-permute-start | bytes 36872 | tf_op jit(solution)/shard_map/ppermute | solution.py:21
  49.2 6.3 %collective-permute-start.7 = (bf16[10,1,768]{2,1,0:T(2,128)(2,1)S(1)}, bf16[10,1,768]{2,1,0:T(2,128)(2,1)S(1)}, u32[]{:S(2)}, u32[]{:S(2)}) collective-permute-start(bf16[10,1,768]{2,1,0:T(2,128)(2,1)S(1)} %get-tuple-element.44), channel_id=1, source_target_pairs={{2,0},{4,2},{6,4},{0,6},{3,1},{5,3},{7,5},{1,7},{10,8},{12,10},{14... | collective-permute-start | bytes 46088 | tf_op jit(solution)/shard_map/ppermute | solution.py:24
  49.6 5.9 %collective-permute-start.6 = (bf16[10,1,768]{2,1,0:T(2,128)(2,1)S(1)}, bf16[10,1,768]{2,1,0:T(2,128)(2,1)S(1)}, u32[]{:S(2)}, u32[]{:S(2)}) collective-permute-start(bf16[10,1,768]{2,1,0:T(2,128)(2,1)S(1)} %get-tuple-element.43), channel_id=1, source_target_pairs={{0,2},{2,4},{4,6},{6,0},{1,3},{3,5},{5,7},{7,1},{8,10},{10,12},{12... | collective-permute-start | bytes 46088 | tf_op jit(solution)/shard_map/ppermute | solution.py:21
  56.0 0.7 copy-start.8
  56.8 5.6 %copy-start.5 = (bf16[256,768]{1,0:T(8,128)(2,1)S(1)}, bf16[256,768]{1,0:T(8,128)(2,1)}, u32[]{:S(2)}) copy-start(bf16[256,768]{1,0:T(8,128)(2,1)} %param.18) | copy-start | bytes 1179652
  61.1 1.4 copy-start.4
  75.9 10.4 %copy-start.7 = (bf16[64,12,64]{0,2,1:T(8,128)(2,1)S(1)}, bf16[64,12,64]{0,2,1:T(8,128)(2,1)}, u32[]{:S(2)}) copy-start(bf16[64,12,64]{0,2,1:T(8,128)(2,1)} %copy.29) | copy-start | bytes 294916
  90.4 21.5 %copy-start.2 = (f32[12,64,4096]{2,1,0:T(8,128)}, f32[12,64,4096]{2,1,0:T(8,128)S(1)}, u32[]{:S(2)}) copy-start(f32[12,64,4096]{2,1,0:T(8,128)S(1)} %get-tuple-element.52) | copy-start | bytes 37748740
  90.5 7.3 %copy-start.3 = (bf16[4096,12,64]{0,2,1:T(8,128)(2,1)S(1)}, bf16[4096,12,64]{0,2,1:T(8,128)(2,1)}, u32[]{:S(2)}) copy-start(bf16[4096,12,64]{0,2,1:T(8,128)(2,1)} %reshape_reshape.11) | copy-start | bytes 18874372
  90.5 7.3 %copy-start.9 = (bf16[64,12,64]{2,1,0:T(8,128)(2,1)S(1)}, bf16[64,12,64]{2,1,0:T(8,128)(2,1)}, u32[]{:S(2)}) copy-start(bf16[64,12,64]{2,1,0:T(8,128)(2,1)} %copy-done.8) | copy-start | bytes 294916
  105.0 6.9 %copy-start.11 = (bf16[64,12,64]{0,2,1:T(8,128)(2,1)S(1)}, bf16[64,12,64]{0,2,1:T(8,128)(2,1)}, u32[]{:S(2)}) copy-start(bf16[64,12,64]{0,2,1:T(8,128)(2,1)} %copy.24) | copy-start | bytes 294916
  120.3 42.6 %collective-permute-start.1 = (bf16[1,8,768]{2,1,0:T(8,128)(2,1)S(1)}, bf16[1,8,768]{2,1,0:T(8,128)(2,1)S(1)}, u32[]{:S(2)}, u32[]{:S(2)}) collective-permute-start(bf16[1,8,768]{2,1,0:T(8,128)(2,1)S(1)} %get-tuple-element.46), channel_id=1, source_target_pairs={{8,0},{16,8},{24,16},{0,24},{9,1},{17,9},{25,17},{1,25},{10,2},{18... | collective-permute-start | bytes 36872 | tf_op jit(solution)/shard_map/ppermute | solution.py:24
  125.1 37.9 %collective-permute-start = (bf16[1,8,768]{2,1,0:T(8,128)(2,1)S(1)}, bf16[1,8,768]{2,1,0:T(8,128)(2,1)S(1)}, u32[]{:S(2)}, u32[]{:S(2)}) collective-permute-start(bf16[1,8,768]{2,1,0:T(8,128)(2,1)S(1)} %get-tuple-element.45), channel_id=1, source_target_pairs={{0,8},{8,16},{16,24},{24,0},{1,9},{9,17},{17,25},{25,1},{2,10},{10... | collective-permute-start | bytes 36872 | tf_op jit(solution)/shard_map/ppermute | solution.py:21
  154.4 142.8 %copy-start.1 = (bf16[768,768]{1,0:T(8,128)(2,1)S(1)}, bf16[768,768]{1,0:T(8,128)(2,1)}, u32[]{:S(2)}) copy-start(bf16[768,768]{1,0:T(8,128)(2,1)} %param.19) | copy-start | bytes 3538948
  163.0 3.9 %collective-permute-start.3 = (bf16[10,1,768]{2,1,0:T(2,128)(2,1)S(1)}, bf16[10,1,768]{2,1,0:T(2,128)(2,1)S(1)}, u32[]{:S(2)}, u32[]{:S(2)}) collective-permute-start(bf16[10,1,768]{2,1,0:T(2,128)(2,1)S(1)} %get-tuple-element.42), channel_id=1, source_target_pairs={{2,0},{4,2},{6,4},{0,6},{3,1},{5,3},{7,5},{1,7},{10,8},{12,10},{14... | collective-permute-start | bytes 46088 | tf_op jit(solution)/shard_map/ppermute | solution.py:24
  164.2 4.8 %collective-permute-start.2 = (bf16[10,1,768]{2,1,0:T(2,128)(2,1)S(1)}, bf16[10,1,768]{2,1,0:T(2,128)(2,1)S(1)}, u32[]{:S(2)}, u32[]{:S(2)}) collective-permute-start(bf16[10,1,768]{2,1,0:T(2,128)(2,1)S(1)} %get-tuple-element.41), channel_id=1, source_target_pairs={{0,2},{2,4},{4,6},{6,0},{1,3},{3,5},{5,7},{7,1},{8,10},{10,12},{12... | collective-permute-start | bytes 46088 | tf_op jit(solution)/shard_map/ppermute | solution.py:21
Sparse Core Ops, SparseCore 0:
  163.0 130.4 all-reduce.4
where the time goes:
time: 305 us; the launch traced here: 304 us
  waiting for transfers between devices  128 us (42%)
  matrix products  65.6 us (22%)
  local copies, waits for them, and re-layouts  41.2 us (14%)
  blocking collectives  22.9 us (8%)
  starting transfers between devices  16.9 us (6%)
  other arithmetic  15 us (5%)
  between operations  14.9 us (5%)
    psum x1, waiting for transfers between devices, per_device(): in_grad, out_grad = lax.psum((in_grad, out_grad), ('lat', 'lon', 'mem'))  124 us
    unnamed x1, blocking collectives  22.9 us
    dot_general x1, matrix products, mutual_attention_adjoint(): jnp.einsum('hqk,qhd->khd', logit_grad, query_heads, preferred_element_typ...  17.7 us
    another operation x1, local copies, waits for them, and re-layouts, mutual_attention_apply(): lookup_projection_entries.reshape(n_tokens, HEADS, CHANNELS_PER_ATT)  10.4 us
    unnamed x35, local copies, waits for them, and re-layouts  10.3 us
    ppermute x4, starting transfers between devices, extended(): lax.ppermute(lax.slice_in_dim(block, 0, width, axis=dim), axis, backward)  9.16 us
    convert_element_type x1, local copies, waits for them, and re-layouts, per_device(): obs_feat = jnp.dot(hidden_act, outer_perceptron_coeffs, preferred_element...  9 us
    dot_general x1, matrix products, per_device(): jnp.einsum('tc,th->ch', token_blocks.reshape(-1, obs_width), hidden_grad,...  7.53 us
  transfers between devices with their start and end apart: 10, of which 3 were waited for; matrix products, arithmetic and copies ran while one was open for 15% of the time, Pallas kernels for 0%

commit v1 on v0

--- a/solution.py
+++ b/solution.py
@@ -1,8 +1,11 @@
+import functools
 import math
 
 import jax
 import jax.numpy as jnp
 from jax import lax
+from jax.experimental import pallas as pl
+from jax.experimental.pallas import tpu as pltpu
 from jax.sharding import PartitionSpec as P
 
 HEADS = 12
@@ -119,6 +122,148 @@
     return measured_embedding_adjoint.reshape(n_tokens, HEADS * CHANNELS_PER_ATT).astype(
         jnp.bfloat16
     )
+
+MESH = pl.DeviceIdType.MESH
+
+
+def sum_scratch(n_lat, n_lon, rows, width):
+    half = rows // 2
+    part = half // n_lon
+    return [
+        pltpu.VMEM((rows, width), jnp.bfloat16),
+        pltpu.VMEM((half, width), jnp.bfloat16),
+        pltpu.VMEM((half, width), jnp.float32),
+        pltpu.VMEM((n_lon, part, width), jnp.bfloat16),
+        pltpu.VMEM((n_lon, part, width), jnp.bfloat16),
+        pltpu.VMEM((n_lat, part, width), jnp.bfloat16),
+        pltpu.VMEM((2, half, width), jnp.bfloat16),
+        pltpu.SemaphoreType.DMA((2,)),
+        pltpu.SemaphoreType.DMA((2,)),
+        pltpu.SemaphoreType.DMA((2, n_lon)),
+        pltpu.SemaphoreType.DMA((2, n_lon)),
+        pltpu.SemaphoreType.DMA((n_lat,)),
+        pltpu.SemaphoreType.DMA((n_lat,)),
+    ]
+
+
+def sum_over_devices(total, n_lat, n_lon, scratch):
+    (rounded, from_core, half_sum, to_lon, from_lon, by_lat, whole,
+     core_send, core_recv, lon_send, lon_recv, lat_send, lat_recv) = scratch
+    lat, lon, mem = (lax.axis_index(name) for name in ("lat", "lon", "mem"))
+    other = 1 - mem
+    rows = total.shape[0]
+    half = rows // 2
+    part = half // n_lon
+
+    rounded[...] = total[...].astype(jnp.bfloat16)
+    away = pl.ds(pl.multiple_of(other * half, half), half)
+    copy = pltpu.make_async_remote_copy(
+        src_ref=rounded.at[away], dst_ref=from_core,
+        send_sem=core_send.at[0], recv_sem=core_recv.at[0],
+        device_id=(lat, lon, other), device_id_type=MESH)
+    copy.start()
+    copy.wait()
+    mine = pl.ds(pl.multiple_of(mem * half, half), half)
+    half_sum[...] = total[mine, :] + from_core[...].astype(jnp.float32)
+
+    to_lon[...] = half_sum[...].astype(jnp.bfloat16).reshape(to_lon.shape)
+    copies = []
+    for step in range(1, n_lon):
+        peer = lax.rem(lon + step, n_lon)
+        copy = pltpu.make_async_remote_copy(
+            src_ref=to_lon.at[peer], dst_ref=from_lon.at[step],
+            send_sem=lon_send.at[0, step], recv_sem=lon_recv.at[0, step],
+            device_id=(lat, peer, mem), device_id_type=MESH)
+        copy.start()
+        copies.append(copy)
+    part_sum = half_sum[pl.ds(pl.multiple_of(lon * part, part), part), :]
+    for step, copy in enumerate(copies, 1):
+        copy.wait()
+        part_sum = part_sum + from_lon[step].astype(jnp.float32)
+
+    by_lat[lat] = part_sum.astype(jnp.bfloat16)
+    copies = []
+    for step in range(1, n_lat):
+        peer = lax.rem(lat + step, n_lat)
+        copy = pltpu.make_async_remote_copy(
+            src_ref=by_lat.at[lat], dst_ref=by_lat.at[lat],
+            send_sem=lat_send.at[step], recv_sem=lat_recv.at[step],
+            device_id=(peer, lon, mem), device_id_type=MESH)
+        copy.start()
+        copies.append(copy)
+    for copy in copies:
+        copy.wait()
+    band_sum = by_lat[0].astype(jnp.float32)
+    for index in range(1, n_lat):
+        band_sum = band_sum + by_lat[index].astype(jnp.float32)
+
+    own = pl.ds(pl.multiple_of(lon * part, part), part)
+    whole[mem, own, :] = band_sum.astype(jnp.bfloat16)
+    copies = []
+    for step in range(1, n_lon):
+        peer = lax.rem(lon + step, n_lon)
+        copy = pltpu.make_async_remote_copy(
+            src_ref=whole.at[mem, own], dst_ref=whole.at[mem, own],
+            send_sem=lon_send.at[1, step], recv_sem=lon_recv.at[1, step],
+            device_id=(lat, peer, mem), device_id_type=MESH)
+        copy.start()
+        copies.append(copy)
+    for copy in copies:
+        copy.wait()
+    copy = pltpu.make_async_remote_copy(
+        src_ref=whole.at[mem], dst_ref=whole.at[mem],
+        send_sem=core_send.at[1], recv_sem=core_recv.at[1],
+        device_id=(lat, lon, other), device_id_type=MESH)
+    copy.start()
+    copy.wait()
+    return whole
+
+
+def greet(partners):
+    barrier = pltpu.get_barrier_semaphore()
+    for partner in partners:
+        pl.semaphore_signal(barrier, inc=1, device_id=partner, device_id_type=MESH)
+    pl.semaphore_wait(barrier, len(partners))
+
+
+def sum_partners(n_lat, n_lon):
+    lat, lon, mem = (lax.axis_index(name) for name in ("lat", "lon", "mem"))
+    partners = [(lat, lon, 1 - mem)]
+    partners += [(lat, lax.rem(lon + step, n_lon), mem) for step in range(1, n_lon)]
+    partners += [(lax.rem(lat + step, n_lat), lon, mem) for step in range(1, n_lat)]
+    return partners
+
+
+def sum_kernel(n_lat, n_lon, in_ref, out_ref, in_sum, out_sum, total, *scratch):
+    greet(sum_partners(n_lat, n_lon))
+    rows, wide = in_ref.shape
+    total[:rows, :wide] = in_ref[...]
+    total[:rows, wide:] = out_ref[:, :wide]
+    total[rows:, :] = out_ref[:, wide:]
+    whole = sum_over_devices(total, n_lat, n_lon, scratch)
+    in_sum[...] = whole[0, :, :wide].astype(jnp.float32)
+    out_sum[:, :wide] = whole[0, :, wide:].astype(jnp.float32)
+    out_sum[:, wide:] = whole[1].astype(jnp.float32)
+
+
+def summed(in_grad, out_grad):
+    n_lat, n_lon = lax.axis_size("lat"), lax.axis_size("lon")
+    rows, width = 2 * in_grad.shape[0], 2 * in_grad.shape[1]
+    return pl.pallas_call(
+        functools.partial(sum_kernel, n_lat, n_lon),
+        out_shape=[
+            jax.ShapeDtypeStruct(in_grad.shape, jnp.float32),
+            jax.ShapeDtypeStruct(out_grad.shape, jnp.float32),
+        ],
+        in_specs=[pl.BlockSpec(memory_space=pltpu.VMEM)] * 2,
+        out_specs=[pl.BlockSpec(memory_space=pltpu.VMEM)] * 2,
+        scratch_shapes=[pltpu.VMEM((rows, width), jnp.float32)]
+        + sum_scratch(n_lat, n_lon, rows, width),
+        compiler_params=pltpu.CompilerParams(
+            collective_id=0, has_side_effects=True, vmem_limit_bytes=32 << 20
+        ),
+        name="sum_over_devices",
+    )(in_grad, out_grad)
 
 
 def per_device(
@@ -221,7 +366,7 @@
         hidden_grad,
         preferred_element_type=jnp.float32,
     )
-    in_grad, out_grad = lax.psum((in_grad, out_grad), ("lat", "lon", "mem"))
+    in_grad, out_grad = summed(in_grad, out_grad)
     return (analysis, in_grad, out_grad)
 
 

time: 305 us -> 187 us (0.61)
  waiting for transfers between devices: 128 us -> 0.02 us
  Pallas kernels: 0 us -> 23 us
  between operations: 14.9 us -> 1.87 us
    psum x1 -> x0, waiting for transfers between devices: 124 us -> none  [per_device(): in_grad, out_grad = lax.psum((in_grad, out_grad), ('lat', 'lon', 'mem'))]
    pallas_call x0 -> x1, Pallas kernels: none -> 23 us  [summed(): pl.pallas_call(functools.partial(sum_kernel, n_lat, n_lon), out_shape=[ja...]
    unnamed x35 -> x79, local copies, waits for them, and re-layouts: 10.3 us -> 10.8 us
  transfers between devices with their start and end apart: 10 -> 9, of which waited for: 3 -> 0; matrix products, arithmetic and copies ran while one was open for 15% -> 25% of each run, Pallas kernels for 0% -> 12%
where the time goes in v1:
time: 187 us; the launch traced here: 186 us
  matrix products  64.7 us (35%)
  local copies, waits for them, and re-layouts  42.9 us (23%)
  Pallas kernels  23 us (12%)
  blocking collectives  20.7 us (11%)
  starting transfers between devices  16.8 us (9%)
  other arithmetic  16.2 us (9%)
  between operations  1.87 us (1%)
    pallas_call x1, Pallas kernels, summed(): pl.pallas_call(functools.partial(sum_kernel, n_lat, n_lon), out_shape=[ja...  23 us
    unnamed x1, blocking collectives  20.7 us
    dot_general x1, matrix products, mutual_attention_adjoint(): jnp.einsum('hqk,qhd->khd', logit_grad, query_heads, preferred_element_typ...  17.7 us
    unnamed x79, local copies, waits for them, and re-layouts  10.8 us
    another operation x1, local copies, waits for them, and re-layouts, mutual_attention_apply(): lookup_projection_entries.reshape(n_tokens, HEADS, CHANNELS_PER_ATT)  10.3 us
    ppermute x4, starting transfers between devices, extended(): lax.ppermute(lax.slice_in_dim(block, 0, width, axis=dim), axis, backward)  9.04 us
    convert_element_type x1, local copies, waits for them, and re-layouts, per_device(): obs_feat = jnp.dot(hidden_act, outer_perceptron_coeffs, preferred_element...  8.99 us
    dot_general x1, matrix products, mutual_attention_adjoint(): jnp.einsum('qhd,khd->hqk', grad_heads, key_heads, preferred_element_type=...  7.26 us
  transfers between devices with their start and end apart: 9, of which 0 were waited for; matrix products, arithmetic and copies ran while one was open for 25% of the time, Pallas kernels for 12%

profile of v1, /device:TPU:0, one launch (start us, length us, event | category | flops | bytes accessed | tf_op | source)
XLA Modules:
  0.0 186.1 jit_solution(18004295114327490187)
XLA Ops:
  3.1 1.6 broadcast_in_dim.20
  4.7 3.4 %scatter_fusion = bf16[32,128,256]{2,1,0:T(8,128)(2,1)} fusion(bf16[32,128,256]{2,1,0:T(8,128)(2,1)} %broadcast_in_dim.20, s32[16]{0:T(128)S(1)} %compare_select_fusion, bf16[16,128,256]{2,1,0:T(8,128)(2,1)} %param.13), kind=kCustom, calls=%fused_computation | custom fusion | bytes 3145792 | tf_op jit(solution)/shard_map/scatter | solution.py:312
  8.1 5.2 %all-to-all-start = ((bf16[4,8,128,256]{3,2,1,0:T(8,128)(2,1)}), bf16[4,8,128,256]{3,2,1,0:T(8,128)(2,1)S(1)}, u32[]{:S(2)}, u32[]{:S(2)}) async-start(bf16[4,8,128,256]{3,2,1,0:T(8,128)(2,1)} %bitcast.5), calls=%async_computation | async-start | bytes 4194304 | tf_op jit(solution)/shard_map/all_to_all | solution.py:315
  13.2 3.6 %collective-permute-start.5 = (bf16[1,8,768]{2,1,0:T(8,128)(2,1)S(1)}, bf16[1,8,768]{2,1,0:T(8,128)(2,1)S(1)}, u32[]{:S(2)}, u32[]{:S(2)}) collective-permute-start(bf16[1,8,768]{2,1,0:T(8,128)(2,1)S(1)} %get-tuple-element.50), channel_id=1, source_target_pairs={{8,0},{16,8},{24,16},{0,24},{9,1},{17,9},{25,17},{1,25},{10,2},{18... | collective-permute-start | bytes 36872 | tf_op jit(solution)/shard_map/ppermute | solution.py:27
  16.9 1.2 dynamic-slice.12
  19.3 1.3 dynamic-update-slice.6
  20.6 20.7 %all-reduce.1 = s32[64]{0:T(128)S(1)} all-reduce(s32[64]{0:T(128)} %dynamic-update-slice.6), channel_id=1, replica_groups=mesh['lat'=4,'lon'=4,'mem'=2] {'lon'}, use_global_device_ids=true, to_apply=%add.1 | all-reduce | flops 64 | bytes 512
  42.6 1.2 broadcast_multiply_fusion
  44.2 1.7 collective-permute-start.6
  46.1 1.1 reshape_reshape.12
  48.1 1.1 reshape.144
  49.5 1.0 convert_multiply_fusion.2
  51.5 4.2 %multiply_convert_fusion.2 = (bf16[4,8,128,256]{3,2,1,0:T(8,128)(2,1)S(1)}, f32[4,8,128,256]{3,2,1,0:T(8,128)}) fusion(bf16[4,8,128,256]{3,2,1,0:T(8,128)(2,1)S(1)} %all-to-all-done, bf16[256,256]{1,0:T(8,128)(2,1)} %param.17), kind=kOutput, calls=%fused_computation.20 | convolution fusion | flops 542113792 | bytes 8519680 | tf_op jit(solution)/shard_map/dot_general | solution.py:316
  55.7 1.4 copy-done.4
  57.1 4.4 %convolution_convert_fusion = bf16[4,8,128,768]{3,2,1,0:T(8,128)(2,1)} fusion(bf16[4,8,128,256]{3,2,1,0:T(8,128)(2,1)S(1)} %get-tuple-element.51, bf16[256,768]{1,0:T(8,128)(2,1)S(1)} %copy-done.5), kind=kOutput, calls=%fused_computation.21 | convolution fusion | flops 1613758464 | bytes 8781824 | tf_op jit(solution)/shard_map/dot_general | solution.py:318
  61.5 9.0 %copy.22 = bf16[4,8,128,768]{2,1,0,3:T(8,128)(2,1)} copy(bf16[4,8,128,768]{3,2,1,0:T(8,128)(2,1)} %convolution_convert_fusion) | data formatting | bytes 12582912 | tf_op jit(solution)/shard_map/convert_element_type | solution.py:320
  70.5 10.3 %reshape_reshape.11 = bf16[4096,12,64]{0,2,1:T(8,128)(2,1)} reshape(bf16[4,8,128,768]{2,1,0,3:T(8,128)(2,1)} %copy.22) | data formatting | bytes 12582912 | tf_op jit(solution)/shard_map/reshape;reshape | solution.py:63
  80.8 4.1 %fusion = (f32[12,64]{1,0:T(8,128)S(1)}, f32[12,64,4096]{2,1,0:T(8,128)S(1)}) fusion(f32[12]{0:T(128)S(1)} %copy-done.32, pred[4096]{0:T(1024)(128)(4,1)S(1)} %broadcast_bitcast_fusion, bf16[64,12,64]{0,2,1:T(8,128)(2,1)S(1)} %copy.29, bf16[4096,12,64]{0,2,1:T(8,128)(2,1)} %reshape_reshape.11), kind=kOutput, calls=%fused_computation.6 | convolution fusion | flops 412089600 | bytes 18979888 | tf_op jit(solution)/shard_map/qhd,khd->hqk/dot_general | solution.py:66
  85.1 3.1 %fusion.2 = f32[12,64]{1,0:T(8,128)S(1)} fusion(f32[12,64,4096]{2,1,0:T(8,128)S(1)} %get-tuple-element.54, f32[12,64]{1,0:T(8,128)S(1)} %multiply_maximum_fusion, f32[12]{0:T(128)S(1)} %copy-done.32, pred[4096]{0:T(1024)(128)(4,1)S(1)} %broadcast_bitcast_fusion), kind=kLoop, calls=%fused_computation.8 | loop fusion | flops 12582144 | bytes 12593200 | tf_op jit(solution)/shard_map/reduce_sum | solution.py:77
  88.3 4.1 %copy-done.3 = bf16[4096,12,64]{0,2,1:T(8,128)(2,1)S(1)} copy-done((bf16[4096,12,64]{0,2,1:T(8,128)(2,1)S(1)}, bf16[4096,12,64]{0,2,1:T(8,128)(2,1)}, u32[]{:S(2)}) %copy-start.3) | copy-done | bytes 6291480
  92.3 7.3 %multiply_reduce_fusion = (f32[12,64]{1,0:T(8,128)S(1)}, f32[12,64,4096]{2,1,0:T(8,128)}) fusion(f32[12,64]{1,0:T(8,128)S(1)} %fusion.53, f32[12,64]{1,0:T(8,128)S(1)} %multiply_maximum_fusion, f32[12,64,4096]{2,1,0:T(8,128)S(1)} %get-tuple-element.54, f32[12]{0:T(128)S(1)} %copy-done.32, pred[4096]{0:T(1024)(128)(4,1)S(1)} %broadcast_bitcast_fusion, ...), kind=kOutput, calls=%fused_computation.3 | convolution fusion | flops 421526784 | bytes 31568944 | tf_op jit(solution)/shard_map/qhd,khd->hqk/dot_general | solution.py:106
  99.6 6.8 %fusion.11 = f32[12,64,4096]{2,1,0:T(8,128)} fusion(bf16[64,12,64]{2,1,0:T(8,128)(2,1)S(1)} %reshape_reshape.13, f32[12,64,4096]{2,1,0:T(8,128)S(1)} %get-tuple-element.54, f32[12,64]{1,0:T(8,128)S(1)} %fusion.53, f32[12,64]{1,0:T(8,128)S(1)} %multiply_maximum_fusion, f32[12]{0:T(128)S(1)} %copy-done.32, pred[4096]{0:T(1024)(128)(4,1)S(1)} %broadcast_bitcast_fusion), kind=kOutput, calls=%fused_computation.22 | convolution fusion | flops 418381824 | bytes 25274416 | tf_op jit(solution)/shard_map/hqk,qhd->khd/dot_general | solution.py:116
  106.5 7.2 %fusion.18 = f32[64,12,64]{0,2,1:T(8,128)} fusion(bf16[4096,12,64]{0,2,1:T(8,128)(2,1)} %reshape_reshape.11, bf16[64,12,64]{0,2,1:T(8,128)(2,1)S(1)} %copy-done.12, f32[64,12]{0,1:T(8,128)S(1)} %convert_bitcast_fusion, f32[12,64,4096]{2,1,0:T(8,128)S(1)} %get-tuple-element.54, f32[12,64]{1,0:T(8,128)S(1)} %fusion.53, ...), kind=kOutput, calls=%fused_computation.27 | convolution fusion | flops 418529280 | bytes 19182640 | tf_op jit(solution)/shard_map/hqk,khd->qhd/dot_general | solution.py:82
  113.7 1.3 copy.26
  115.0 1.8 copy.25
  117.8 3.8 %collective-permute-start.1 = (bf16[1,8,768]{2,1,0:T(8,128)(2,1)S(1)}, bf16[1,8,768]{2,1,0:T(8,128)(2,1)S(1)}, u32[]{:S(2)}, u32[]{:S(2)}) collective-permute-start(bf16[1,8,768]{2,1,0:T(8,128)(2,1)S(1)} %get-tuple-element.48), channel_id=1, source_target_pairs={{8,0},{16,8},{24,16},{0,24},{9,1},{17,9},{25,17},{1,25},{10,2},{18... | collective-permute-start | bytes 36872 | tf_op jit(solution)/shard_map/ppermute | solution.py:27
  122.4 5.5 %fusion.10 = f32[4096,256]{1,0:T(8,128)} fusion(f32[4,8,128,256]{3,2,1,0:T(8,128)} %get-tuple-element.52), kind=kLoop, calls=%fused_computation.19 | loop fusion | flops 7340032 | bytes 8388608 | tf_op jit(solution)/shard_map/mul | solution.py:34
  127.9 17.7 %add_convert_fusion = bf16[12,64,4096]{2,1,0:T(8,128)(2,1)} fusion(f32[12,64,4096]{2,1,0:T(8,128)} %fusion.11, bf16[64,12,64]{0,2,1:T(8,128)(2,1)S(1)} %copy-done.9, f32[12,64,4096]{2,1,0:T(8,128)} %get-tuple-element.56, f32[12,64]{1,0:T(8,128)S(1)} %get-tuple-element.41, f32[12]{0:T(128)S(1)} %copy-done.32, f32[12,64,4096]{2,1,0:T(8,128)} %copy-done.2, ...), kind=kOutput, calls=%fused_computation.1 | convolution fusion | flops 434110464 | bytes 44151856 | tf_op jit(solution)/shard_map/hqk,qhd->khd/dot_general | solution.py:119
  145.6 6.7 %fusion.21.in_ref = f32[256,256]{1,0:T(8,128)S(1)} fusion(bf16[4096,256]{1,0:T(8,128)(2,1)S(1)} %bitcast.90, f32[4096,256]{1,0:T(8,128)} %fusion.10, bf16[4096,768]{0,1:T(8,128)(2,1)} %bitcast.91, bf16[256,768]{1,0:T(8,128)(2,1)S(1)} %copy-done.5), kind=kOutput, calls=%fused_computation.29 | convolution fusion | flops 2149580800 | bytes 13238272 | tf_op jit(solution)/shard_map/tc,th->ch/dot_general | solution.py:363
  153.0 1.2 collective-permute-start.3
  155.1 5.3 %fusion.58.out_ref = f32[256,768]{1,0:T(8,128)S(1)} fusion(bf16[4096,256]{1,0:T(8,128)(2,1)} %bitcast.93, bf16[4096,768]{0,1:T(8,128)(2,1)} %bitcast.92), kind=kOutput, calls=%fused_computation.114 | convolution fusion | flops 1610612736 | bytes 9175040 | tf_op jit(solution)/shard_map/th,td->hd/dot_general | solution.py:362
  160.5 23.0 %sum_over_devices.1 = (f32[256,256]{1,0:T(8,128)S(1)}, f32[256,768]{1,0:T(8,128)S(1)}) custom-call(f32[256,256]{1,0:T(8,128)S(1)} %fusion.21.in_ref, f32[256,768]{1,0:T(8,128)S(1)} %fusion.58.out_ref), custom_call_target="tpu_custom_call" | custom-call | tf_op jit(solution)/shard_map/sum_over_devices/pallas_call | solution.py:252
  (121 shorter events, 12.9 us)
Async XLA Ops:
  0.6 41.0 %copy-start = (bf16[768,768]{1,0:T(8,128)(2,1)S(1)}, bf16[768,768]{1,0:T(8,128)(2,1)}, u32[]{:S(2)}) copy-start(bf16[768,768]{1,0:T(8,128)(2,1)} %param.19) | copy-start | bytes 3538948
  0.6 18.6 %copy-start.36 = (s32[16]{0:T(128)S(1)}, s32[16]{0:T(128)}, u32[]{:S(2)}) copy-start(s32[16]{0:T(128)} %param.14) | copy-start | bytes 196
  0.7 12.6 %copy-start.11 = (bf16[1,8,8,768]{3,2,1,0:T(8,128)(2,1)S(1)}, bf16[1,8,8,768]{3,2,1,0:T(8,128)(2,1)}, u32[]{:S(2)}) copy-start(bf16[1,8,8,768]{3,2,1,0:T(8,128)(2,1)} %param.16) | copy-start | bytes 294916
  0.7 40.9 %copy-start.6 = (bf16[1,8,8,768]{3,2,1,0:T(8,128)(2,1)S(1)}, bf16[1,8,8,768]{3,2,1,0:T(8,128)(2,1)}, u32[]{:S(2)}) copy-start(bf16[1,8,8,768]{3,2,1,0:T(8,128)(2,1)} %param.15) | copy-start | bytes 294916
  0.7 45.2 %copy-start.33 = (f32[8,768]{1,0:T(8,128)S(1)}, f32[8,768]{1,0:T(8,128)}, u32[]{:S(2)}) copy-start(f32[8,768]{1,0:T(8,128)} %param.21) | copy-start | bytes 73732
  8.1 43.4 %all-to-all-start = ((bf16[4,8,128,256]{3,2,1,0:T(8,128)(2,1)}), bf16[4,8,128,256]{3,2,1,0:T(8,128)(2,1)S(1)}, u32[]{:S(2)}, u32[]{:S(2)}) async-start(bf16[4,8,128,256]{3,2,1,0:T(8,128)(2,1)} %bitcast.5), calls=%async_computation | async-start | bytes 4194304 | tf_op jit(solution)/shard_map/all_to_all | solution.py:315
  13.2 30.5 %collective-permute-start.5 = (bf16[1,8,768]{2,1,0:T(8,128)(2,1)S(1)}, bf16[1,8,768]{2,1,0:T(8,128)(2,1)S(1)}, u32[]{:S(2)}, u32[]{:S(2)}) collective-permute-start(bf16[1,8,768]{2,1,0:T(8,128)(2,1)S(1)} %get-tuple-element.50), channel_id=1, source_target_pairs={{8,0},{16,8},{24,16},{0,24},{9,1},{17,9},{25,17},{1,25},{10,2},{18... | collective-permute-start | bytes 36872 | tf_op jit(solution)/shard_map/ppermute | solution.py:27
  16.9 26.9 %collective-permute-start.4 = (bf16[1,8,768]{2,1,0:T(8,128)(2,1)S(1)}, bf16[1,8,768]{2,1,0:T(8,128)(2,1)S(1)}, u32[]{:S(2)}, u32[]{:S(2)}) collective-permute-start(bf16[1,8,768]{2,1,0:T(8,128)(2,1)S(1)} %get-tuple-element.49), channel_id=1, source_target_pairs={{0,8},{8,16},{16,24},{24,0},{1,9},{9,17},{17,25},{25,1},{2,10},{10... | collective-permute-start | bytes 36872 | tf_op jit(solution)/shard_map/ppermute | solution.py:24
  43.8 5.7 %collective-permute-start.7 = (bf16[10,1,768]{2,1,0:T(2,128)(2,1)S(1)}, bf16[10,1,768]{2,1,0:T(2,128)(2,1)S(1)}, u32[]{:S(2)}, u32[]{:S(2)}) collective-permute-start(bf16[10,1,768]{2,1,0:T(2,128)(2,1)S(1)} %get-tuple-element.46), channel_id=1, source_target_pairs={{2,0},{4,2},{6,4},{0,6},{3,1},{5,3},{7,5},{1,7},{10,8},{12,10},{14... | collective-permute-start | bytes 46088 | tf_op jit(solution)/shard_map/ppermute | solution.py:27
  44.2 5.3 %collective-permute-start.6 = (bf16[10,1,768]{2,1,0:T(2,128)(2,1)S(1)}, bf16[10,1,768]{2,1,0:T(2,128)(2,1)S(1)}, u32[]{:S(2)}, u32[]{:S(2)}) collective-permute-start(bf16[10,1,768]{2,1,0:T(2,128)(2,1)S(1)} %get-tuple-element.45), channel_id=1, source_target_pairs={{0,2},{2,4},{4,6},{6,0},{1,3},{3,5},{5,7},{7,1},{8,10},{10,12},{12... | collective-permute-start | bytes 46088 | tf_op jit(solution)/shard_map/ppermute | solution.py:24
  49.4 31.4 %copy-start.8 = (bf16[64,12,64]{0,2,1:T(8,128)(2,1)}, bf16[64,12,64]{0,2,1:T(8,128)(2,1)S(1)}, u32[]{:S(2)}) copy-start(bf16[64,12,64]{0,2,1:T(8,128)(2,1)S(1)} %copy.29) | copy-start | bytes 294916
  70.5 10.3 %copy-start.32 = (f32[12]{0:T(128)S(1)}, f32[12]{0:T(128)}, u32[]{:S(2)}) copy-start(f32[12]{0:T(128)} %broadcast_multiply_fusion) | copy-start | bytes 148
  85.0 21.5 %copy-start.2 = (f32[12,64,4096]{2,1,0:T(8,128)}, f32[12,64,4096]{2,1,0:T(8,128)S(1)}, u32[]{:S(2)}) copy-start(f32[12,64,4096]{2,1,0:T(8,128)S(1)} %get-tuple-element.54) | copy-start | bytes 37748740
  85.1 7.3 %copy-start.3 = (bf16[4096,12,64]{0,2,1:T(8,128)(2,1)S(1)}, bf16[4096,12,64]{0,2,1:T(8,128)(2,1)}, u32[]{:S(2)}) copy-start(bf16[4096,12,64]{0,2,1:T(8,128)(2,1)} %reshape_reshape.11) | copy-start | bytes 18874372
  99.6 6.9 %copy-start.12 = (bf16[64,12,64]{0,2,1:T(8,128)(2,1)S(1)}, bf16[64,12,64]{0,2,1:T(8,128)(2,1)}, u32[]{:S(2)}) copy-start(bf16[64,12,64]{0,2,1:T(8,128)(2,1)} %copy.24) | copy-start | bytes 294916
  106.4 10.4 %copy-start.7 = (bf16[1,8,8,768]{3,2,1,0:T(8,128)(2,1)S(1)}, bf16[1,8,8,768]{3,2,1,0:T(8,128)(2,1)}, u32[]{:S(2)}) copy-start(bf16[1,8,8,768]{3,2,1,0:T(8,128)(2,1)} %param.15) | copy-start | bytes 294916
  113.6 14.3 %copy-start.9 = (bf16[64,12,64]{0,2,1:T(8,128)(2,1)S(1)}, bf16[64,12,64]{0,2,1:T(8,128)(2,1)}, u32[]{:S(2)}) copy-start(bf16[64,12,64]{0,2,1:T(8,128)(2,1)} %copy-done.8) | copy-start | bytes 294916
  117.8 34.5 %collective-permute-start.1 = (bf16[1,8,768]{2,1,0:T(8,128)(2,1)S(1)}, bf16[1,8,768]{2,1,0:T(8,128)(2,1)S(1)}, u32[]{:S(2)}, u32[]{:S(2)}) collective-permute-start(bf16[1,8,768]{2,1,0:T(8,128)(2,1)S(1)} %get-tuple-element.48), channel_id=1, source_target_pairs={{8,0},{16,8},{24,16},{0,24},{9,1},{17,9},{25,17},{1,25},{10,2},{18... | collective-permute-start | bytes 36872 | tf_op jit(solution)/shard_map/ppermute | solution.py:27
  122.4 29.9 %collective-permute-start = (bf16[1,8,768]{2,1,0:T(8,128)(2,1)S(1)}, bf16[1,8,768]{2,1,0:T(8,128)(2,1)S(1)}, u32[]{:S(2)}, u32[]{:S(2)}) collective-permute-start(bf16[1,8,768]{2,1,0:T(8,128)(2,1)S(1)} %get-tuple-element.47), channel_id=1, source_target_pairs={{0,8},{8,16},{16,24},{24,0},{1,9},{9,17},{17,25},{25,1},{2,10},{10... | collective-permute-start | bytes 36872 | tf_op jit(solution)/shard_map/ppermute | solution.py:24
  153.0 30.5 %collective-permute-start.3 = (bf16[10,1,768]{2,1,0:T(2,128)(2,1)S(1)}, bf16[10,1,768]{2,1,0:T(2,128)(2,1)S(1)}, u32[]{:S(2)}, u32[]{:S(2)}) collective-permute-start(bf16[10,1,768]{2,1,0:T(2,128)(2,1)S(1)} %get-tuple-element.44), channel_id=1, source_target_pairs={{2,0},{4,2},{6,4},{0,6},{3,1},{5,3},{7,5},{1,7},{10,8},{12,10},{14... | collective-permute-start | bytes 46088 | tf_op jit(solution)/shard_map/ppermute | solution.py:27
  154.2 29.3 %collective-permute-start.2 = (bf16[10,1,768]{2,1,0:T(2,128)(2,1)S(1)}, bf16[10,1,768]{2,1,0:T(2,128)(2,1)S(1)}, u32[]{:S(2)}, u32[]{:S(2)}) collective-permute-start(bf16[10,1,768]{2,1,0:T(2,128)(2,1)S(1)} %get-tuple-element.43), channel_id=1, source_target_pairs={{0,2},{2,4},{4,6},{6,0},{1,3},{3,5},{5,7},{7,1},{8,10},{10,12},{12... | collective-permute-start | bytes 46088 | tf_op jit(solution)/shard_map/ppermute | solution.py:24
  155.0 31.1 %copy-start.1 = (bf16[768,768]{1,0:T(8,128)(2,1)S(1)}, bf16[768,768]{1,0:T(8,128)(2,1)}, u32[]{:S(2)}) copy-start(bf16[768,768]{1,0:T(8,128)(2,1)} %param.19) | copy-start | bytes 3538948
  155.0 28.4 %copy-start.15 = (bf16[1,8,768]{2,1,0:T(8,128)(2,1)S(1)}, bf16[1,8,768]{2,1,0:T(8,128)(2,1)}, u32[]{:S(2)}) copy-start(bf16[1,8,768]{2,1,0:T(8,128)(2,1)} %copy-done.14) | copy-start | bytes 36868
  155.1 28.5 %copy-start.35 = (f32[10]{0:T(128)S(1)}, f32[10]{0:T(128)}, u32[]{:S(2)}) copy-start(f32[10]{0:T(128)} %copy-done.34) | copy-start | bytes 124
  155.1 28.6 %copy-start.17 = (f32[768]{0:T(1024)S(1)}, f32[768]{0:T(1024)}, u32[]{:S(2)}) copy-start(f32[768]{0:T(1024)} %copy-done.16) | copy-start | bytes 9220
  155.1 28.6 %copy-start.19 = (f32[768]{0:T(1024)S(1)}, f32[768]{0:T(1024)}, u32[]{:S(2)}) copy-start(f32[768]{0:T(1024)} %copy-done.18) | copy-start | bytes 9220
  155.1 28.6 %copy-start.21 = (f32[768]{0:T(1024)S(1)}, f32[768]{0:T(1024)}, u32[]{:S(2)}) copy-start(f32[768]{0:T(1024)} %copy-done.20) | copy-start | bytes 9220
  155.1 28.6 %copy-start.23 = (f32[768]{0:T(1024)S(1)}, f32[768]{0:T(1024)}, u32[]{:S(2)}) copy-start(f32[768]{0:T(1024)} %copy-done.22) | copy-start | bytes 9220
  155.1 28.6 %copy-start.25 = (f32[768]{0:T(1024)S(1)}, f32[768]{0:T(1024)}, u32[]{:S(2)}) copy-start(f32[768]{0:T(1024)} %copy-done.24) | copy-start | bytes 9220
  155.1 28.6 %copy-start.27 = (f32[768]{0:T(1024)S(1)}, f32[768]{0:T(1024)}, u32[]{:S(2)}) copy-start(f32[768]{0:T(1024)} %copy-done.26) | copy-start | bytes 9220
  155.1 28.6 %copy-start.29 = (f32[768]{0:T(1024)S(1)}, f32[768]{0:T(1024)}, u32[]{:S(2)}) copy-start(f32[768]{0:T(1024)} %copy-done.28) | copy-start | bytes 9220
  155.1 28.6 %copy-start.31 = (f32[768]{0:T(1024)S(1)}, f32[768]{0:T(1024)}, u32[]{:S(2)}) copy-start(f32[768]{0:T(1024)} %copy-done.30) | copy-start | bytes 9220
  (14 other events, 60.0 us)

commit v2 on v1

v2 whole, which is shorter than its diff:
```python
import functools
import math

import jax
import jax.numpy as jnp
from jax import lax
from jax.experimental import pallas as pl
from jax.experimental.pallas import tpu as pltpu
from jax.sharding import PartitionSpec as P

HEADS = 12
CHANNELS_PER_ATT = 64
GROUP = 256
CHUNK = 512
LOWEST = -1e30


NEIGHBOURS = ((-1, -1), (-1, 0), (-1, 1), (0, -1), (0, 1), (1, -1), (1, 0), (1, 1))

MESH = pl.DeviceIdType.MESH


def sum_scratch(n_lat, n_lon, rows, width):
    half = rows // 2
    part = half // n_lon
    return [
        pltpu.VMEM((rows, width), jnp.bfloat16),
        pltpu.VMEM((half, width), jnp.bfloat16),
        pltpu.VMEM((half, width), jnp.float32),
        pltpu.VMEM((n_lon, part, width), jnp.bfloat16),
        pltpu.VMEM((n_lon, part, width), jnp.bfloat16),
        pltpu.VMEM((n_lat, part, width), jnp.bfloat16),
        pltpu.VMEM((2, half, width), jnp.bfloat16),
        pltpu.SemaphoreType.DMA((2,)),
        pltpu.SemaphoreType.DMA((2,)),
        pltpu.SemaphoreType.DMA((2, n_lon)),
        pltpu.SemaphoreType.DMA((2, n_lon)),
        pltpu.SemaphoreType.DMA((n_lat,)),
        pltpu.SemaphoreType.DMA((n_lat,)),
    ]


def sum_over_devices(total, n_lat, n_lon, scratch):
    (rounded, from_core, half_sum, to_lon, from_lon, by_lat, whole,
     core_send, core_recv, lon_send, lon_recv, lat_send, lat_recv) = scratch
    lat, lon, mem = (lax.axis_index(name) for name in ("lat", "lon", "mem"))
    other = 1 - mem
    rows = total.shape[0]
    half = rows // 2
    part = half // n_lon

    rounded[...] = total[...].astype(jnp.bfloat16)
    away = pl.ds(pl.multiple_of(other * half, half), half)
    copy = pltpu.make_async_remote_copy(
        src_ref=rounded.at[away], dst_ref=from_core,
        send_sem=core_send.at[0], recv_sem=core_recv.at[0],
        device_id=(lat, lon, other), device_id_type=MESH)
    copy.start()
    copy.wait()
    mine = pl.ds(pl.multiple_of(mem * half, half), half)
    half_sum[...] = total[mine, :] + from_core[...].astype(jnp.float32)

    to_lon[...] = half_sum[...].astype(jnp.bfloat16).reshape(to_lon.shape)
    copies = []
    for step in range(1, n_lon):
        peer = lax.rem(lon + step, n_lon)
        copy = pltpu.make_async_remote_copy(
            src_ref=to_lon.at[peer], dst_ref=from_lon.at[step],
            send_sem=lon_send.at[0, step], recv_sem=lon_recv.at[0, step],
            device_id=(lat, peer, mem), device_id_type=MESH)
        copy.start()
        copies.append(copy)
    part_sum = half_sum[pl.ds(pl.multiple_of(lon * part, part), part), :]
    for step, copy in enumerate(copies, 1):
        copy.wait()
        part_sum = part_sum + from_lon[step].astype(jnp.float32)

    by_lat[lat] = part_sum.astype(jnp.bfloat16)
    copies = []
    for step in range(1, n_lat):
        peer = lax.rem(lat + step, n_lat)
        copy = pltpu.make_async_remote_copy(
            src_ref=by_lat.at[lat], dst_ref=by_lat.at[lat],
            send_sem=lat_send.at[step], recv_sem=lat_recv.at[step],
            device_id=(peer, lon, mem), device_id_type=MESH)
        copy.start()
        copies.append(copy)
    for copy in copies:
        copy.wait()
    band_sum = by_lat[0].astype(jnp.float32)
    for index in range(1, n_lat):
        band_sum = band_sum + by_lat[index].astype(jnp.float32)

    own = pl.ds(pl.multiple_of(lon * part, part), part)
    whole[mem, own, :] = band_sum.astype(jnp.bfloat16)
    copies = []
    for step in range(1, n_lon):
        peer = lax.rem(lon + step, n_lon)
        copy = pltpu.make_async_remote_copy(
            src_ref=whole.at[mem, own], dst_ref=whole.at[mem, own],
            send_sem=lon_send.at[1, step], recv_sem=lon_recv.at[1, step],
            device_id=(lat, peer, mem), device_id_type=MESH)
        copy.start()
        copies.append(copy)
    for copy in copies:
        copy.wait()
    copy = pltpu.make_async_remote_copy(
        src_ref=whole.at[mem], dst_ref=whole.at[mem],
        send_sem=core_send.at[1], recv_sem=core_recv.at[1],
        device_id=(lat, lon, other), device_id_type=MESH)
    copy.start()
    copy.wait()
    return whole


def greet(partners):
    barrier = pltpu.get_barrier_semaphore()
    for partner in partners:
        pl.semaphore_signal(barrier, inc=1, device_id=partner, device_id_type=MESH)
    pl.semaphore_wait(barrier, len(partners))


def rows_of(index, size):
    return pl.ds(pl.multiple_of(index * size, size), size)


def lanes_of(group):
    return slice(group * GROUP, (group + 1) * GROUP)


def dot(left, right):
    return jnp.dot(left, right, preferred_element_type=jnp.float32)


def dot_rows(left, right):
    return lax.dot_general(
        left, right, (((0,), (0,)), ((), ())), preferred_element_type=jnp.float32
    )


def spread_heads(cells):
    tall = jnp.concatenate([cells] * (GROUP // CHANNELS_PER_ATT), axis=0)
    row_head = lax.broadcasted_iota(jnp.int32, tall.shape, 0) // cells.shape[0]
    col_head = lax.broadcasted_iota(jnp.int32, tall.shape, 1) // CHANNELS_PER_ATT
    return jnp.where(row_head == col_head, tall, 0.0)


def gather_heads(tall, n_cells):
    col_head = lax.broadcasted_iota(jnp.int32, (n_cells, GROUP), 1) // CHANNELS_PER_ATT
    cells = tall[:n_cells]
    for head in range(1, GROUP // CHANNELS_PER_ATT):
        cells = jnp.where(col_head == head, tall[head * n_cells : (head + 1) * n_cells], cells)
    return cells


def step_kernel(
    n_lat, n_lon, n_blocks, grid_rows, grid_cols,
    targets, tokens, latent, cotangent, inner, outer, projector, sharpness, mixing,
    analysis, in_sum, out_sum,
    latents, cots, cots_above, cots_below, band, outer_t,
    query_rows, query_cols, grad_rows, grad_cols, self_rows,
    features, hidden, slope, block_stats, stats, tile_stats,
    update, update_out, update_in, state, side, rims_out, rims_in, padded, total,
    lat_send, lat_recv, cot_send, cot_recv, rim_send, rim_recv,
    stat_send, stat_recv, up_send, up_recv, halo_send, halo_recv,
    *sum_refs,
):
    lat, lon, mem = (lax.axis_index(name) for name in ("lat", "lon", "mem"))
    n_cells, width = latent.shape
    grads = update
    n_tokens = tokens.shape[0]
    block_len = n_tokens // n_blocks
    groups = width // GROUP
    above, below = lax.rem(lat + n_lat - 1, n_lat), lax.rem(lat + 1, n_lat)
    keep_above = jnp.where(lat > 0, 1.0, 0.0)
    keep_below = jnp.where(lat < n_lat - 1, 1.0, 0.0)
    sectors = [lax.rem(lon + step, n_lon) for step in range(n_lon)]

    partners = [(lat, lon, 1 - mem)]
    partners += [(lat, sector, mem) for sector in sectors[1:]]
    partners += [(row, sector, mem) for row in (above, below) for sector in sectors]
    partners += [(lax.rem(lat + step, n_lat), lon, mem) for step in range(2, n_lat - 1)]
    greet(partners)

    def send(src, dst, send_sem, recv_sem, device):
        copy = pltpu.make_async_remote_copy(
            src_ref=src, dst_ref=dst, send_sem=send_sem, recv_sem=recv_sem,
            device_id=device, device_id_type=MESH)
        copy.start()
        return copy

    arriving = []
    for step in range(1, n_lon):
        arriving.append(send(latent, latents.at[lon], lat_send.at[step], lat_recv.at[step],
                             (lat, sectors[step], mem)))
    for step in range(1, n_lon):
        arriving.append(send(cotangent, cots.at[lon], cot_send.at[step], cot_recv.at[step],
                             (lat, sectors[step], mem)))
    for step in range(n_lon):
        arriving.append(send(cotangent.at[pl.ds(n_cells - 16, 16)], cots_above.at[lon],
                             rim_send.at[0, step], rim_recv.at[0, step],
                             (below, sectors[step], mem)))
        arriving.append(send(cotangent.at[pl.ds(0, 16)], cots_below.at[lon],
                             rim_send.at[1, step], rim_recv.at[1, step],
                             (above, sectors[step], mem)))
    latents[lon] = latent[...]
    cots[lon] = cotangent[...]
    outer_t[...] = outer[...].astype(jnp.float32).T.astype(jnp.bfloat16)

    def perceptron(index, carry):
        rows = rows_of(index, CHUNK)
        pre_act = dot(tokens[rows, :], inner[...])
        sigmoid_val = jax.nn.sigmoid(pre_act)
        slope[rows, :] = sigmoid_val * (1.0 + pre_act * (1.0 - sigmoid_val))
        hidden_act = (pre_act * sigmoid_val).astype(jnp.bfloat16)
        hidden[rows, :] = hidden_act
        features[rows, :] = dot(hidden_act, outer[...]).astype(jnp.bfloat16)
        return carry

    lax.fori_loop(0, n_tokens // CHUNK, perceptron, 0)
    for copy in arriving:
        copy.wait()

    for tile in range(n_lon):
        cols = slice(tile * grid_cols, (tile + 1) * grid_cols)
        band[1 : 1 + grid_rows, cols, :] = (
            cots[tile].astype(jnp.float32).reshape(grid_rows, grid_cols, width))
        band[0, cols, :] = cots_above[tile].astype(jnp.float32)[16 - grid_cols :] * keep_above
        band[1 + grid_rows, cols, :] = cots_below[tile].astype(jnp.float32)[:grid_cols] * keep_below

    def mix_row(row, carry):
        for group in range(groups):
            lanes = lanes_of(group)
            mixed = band[1 + row, :, lanes]
            for index, (row_step, col_step) in enumerate(NEIGHBOURS):
                line = band[1 + row - row_step, :, lanes]
                if col_step:
                    line = pltpu.roll(line, col_step % (n_lon * grid_cols), 0)
                mixed = mixed + mixing[index : index + 1, lanes] * line
            mixed = mixed.astype(jnp.bfloat16).astype(jnp.float32)
            for tile in range(n_lon):
                grads[tile, rows_of(row, grid_cols), lanes] = (
                    mixed[tile * grid_cols : (tile + 1) * grid_cols])
        return carry

    lax.fori_loop(0, grid_rows, mix_row, 0)

    def prepare(tile, carry):
        query = dot(latents[tile], projector[...]).astype(jnp.bfloat16).astype(jnp.float32)
        for group in range(groups):
            lanes = lanes_of(group)
            cell_t = spread_heads(latents[tile, :, lanes].astype(jnp.float32)).T
            spread = spread_heads(query[:, lanes])
            spread_t = spread.T
            query_rows[tile, group] = spread.astype(jnp.bfloat16)
            query_cols[tile, group] = spread_t.astype(jnp.bfloat16)
            self_rows[tile, 0:1, lanes] = (
                jnp.sum(spread_t * cell_t, axis=0, keepdims=True) * sharpness[:, lanes])
            spread = spread_heads(grads[tile, :, lanes])
            spread_t = spread.T
            grad_rows[tile, group] = spread.astype(jnp.bfloat16)
            grad_cols[tile, group] = spread_t.astype(jnp.bfloat16)
            self_rows[tile, 1:2, lanes] = jnp.sum(spread_t * cell_t, axis=0, keepdims=True)
        return carry

    lax.fori_loop(0, n_lon, prepare, 0)

    def block_sums(block, carry):
        tile = targets[block]
        rows = rows_of(block, block_len)
        for group in range(groups):
            lanes = lanes_of(group)
            feature = features[rows, lanes]
            scores = dot(feature, query_cols[tile, group]) * sharpness[:, lanes]
            weight_grad = dot(feature, grad_cols[tile, group])
            top = jnp.max(scores, axis=0, keepdims=True)
            exp_terms = jnp.exp(scores - top)
            block_stats[block, 0:1, lanes] = top
            block_stats[block, 1:2, lanes] = jnp.sum(exp_terms, axis=0, keepdims=True)
            block_stats[block, 2:3, lanes] = jnp.sum(
                exp_terms * weight_grad, axis=0, keepdims=True)
        return carry

    lax.fori_loop(0, n_blocks, block_sums, 0)

    for tile in range(n_lon):
        tops = [jnp.where(targets[block] == tile, block_stats[block, 0:1, :], LOWEST)
                for block in range(n_blocks)]
        top = functools.reduce(jnp.maximum, tops)
        exp_sum = jnp.zeros_like(top)
        grad_sum = jnp.zeros_like(top)
        for block in range(n_blocks):
            scale = jnp.exp(tops[block] - top)
            scale = jnp.where(targets[block] == tile, scale, 0.0)
            exp_sum = exp_sum + scale * block_stats[block, 1:2, :]
            grad_sum = grad_sum + scale * block_stats[block, 2:3, :]
        stats[lon, 4 * tile : 4 * tile + 1, :] = top
        stats[lon, 4 * tile + 1 : 4 * tile + 2, :] = exp_sum
        stats[lon, 4 * tile + 2 : 4 * tile + 3, :] = grad_sum
        stats[lon, 4 * tile + 3 : 4 * tile + 4, :] = jnp.zeros_like(top)

    arriving = [
        send(stats.at[lon], stats.at[lon], stat_send.at[step], stat_recv.at[step],
             (lat, sectors[step], mem))
        for step in range(1, n_lon)]
    update[...] = jnp.zeros_like(update)
    total[...] = jnp.zeros_like(total)
    for copy in arriving:
        copy.wait()

    for tile in range(n_lon):
        self_score = self_rows[tile, 0:1, :]
        top = self_score
        for sector in range(n_lon):
            top = jnp.maximum(top, stats[sector, 4 * tile : 4 * tile + 1, :])
        self_exp = jnp.exp(self_score - top)
        exp_sum = self_exp
        grad_sum = self_exp * self_rows[tile, 1:2, :]
        for sector in range(n_lon):
            scale = jnp.exp(stats[sector, 4 * tile : 4 * tile + 1, :] - top)
            exp_sum = exp_sum + scale * stats[sector, 4 * tile + 1 : 4 * tile + 2, :]
            grad_sum = grad_sum + scale * stats[sector, 4 * tile + 2 : 4 * tile + 3, :]
        inverse = 1.0 / exp_sum
        tile_stats[tile, 0:1, :] = top
        tile_stats[tile, 1:2, :] = inverse
        tile_stats[tile, 2:3, :] = grad_sum * inverse
        tile_stats[tile, 3:4, :] = self_exp * inverse

    def attend(block, carry):
        tile = targets[block]
        rows = rows_of(block, block_len)
        for group in range(groups):
            lanes = lanes_of(group)
            feature = features[rows, lanes]
            scores = dot(feature, query_cols[tile, group]) * sharpness[:, lanes]
            weight_grad = dot(feature, grad_cols[tile, group])
            tile_rows = tile_stats[tile, :, lanes]
            probs = jnp.exp(scores - tile_rows[0:1]) * tile_rows[1:2]
            weights = probs.astype(jnp.bfloat16)
            logit_grad = (
                probs * (weight_grad - tile_rows[2:3]) * sharpness[:, lanes]
            ).astype(jnp.bfloat16)
            features[rows, lanes] = (
                dot(weights, grad_rows[tile, group]) + dot(logit_grad, query_rows[tile, group])
            ).astype(jnp.bfloat16)
            part = gather_heads(dot_rows(weights, feature), n_cells)
            for sector in range(n_lon):
                update[sector, :, lanes] += jnp.where(tile == sector, part, 0.0)
        return carry

    lax.fori_loop(0, n_blocks, attend, 0)

    update_out[...] = update[...].astype(jnp.bfloat16)
    arriving = [
        send(update_out.at[sectors[step]], update_in.at[step], up_send.at[step], up_recv.at[step],
             (lat, sectors[step], mem))
        for step in range(1, n_lon)]

    def perceptron_grad(index, carry):
        rows = rows_of(index, CHUNK)
        feature_grad = features[rows, :]
        hidden_grad = (dot(feature_grad, outer_t[...]) * slope[rows, :]).astype(jnp.bfloat16)
        out_grad = dot_rows(hidden[rows, :], feature_grad)
        total[:GROUP, :GROUP] += dot_rows(tokens[rows, :], hidden_grad)
        total[:GROUP, GROUP:] += out_grad[:, :GROUP]
        total[GROUP:, :] += out_grad[:, GROUP:]
        return carry

    lax.fori_loop(0, n_tokens // CHUNK, perceptron_grad, 0)

    for copy in arriving:
        copy.wait()
    own_stats = tile_stats[lon]
    for group in range(groups):
        lanes = lanes_of(group)
        cells = latent[:, lanes].astype(jnp.float32)
        eye_shape = (GROUP, GROUP)
        eye = lax.broadcasted_iota(jnp.int32, eye_shape, 0) == lax.broadcasted_iota(
            jnp.int32, eye_shape, 1)
        self_weight = own_stats[3:4, lanes].astype(jnp.bfloat16).astype(jnp.float32)
        diagonal = jnp.where(eye, self_weight, 0.0).astype(jnp.bfloat16)
        own = dot(diagonal, spread_heads(cells).astype(jnp.bfloat16))
        change = update[lon, :, lanes] + gather_heads(own, n_cells)
        for step in range(1, n_lon):
            change = change + update_in[step, :, lanes].astype(jnp.float32)
        rounded = (cells + change).astype(jnp.bfloat16).astype(jnp.float32)
        state[:, :, lanes] = rounded.reshape(grid_rows, grid_cols, GROUP)
    for row in range(grid_rows):
        side[row : row + 1, :] = state[row, grid_cols - 1 : grid_cols, :]
        side[grid_rows + row : grid_rows + row + 1, :] = state[row, 0:1, :]
    rims_out[0] = state[0:2].reshape(16, width).astype(jnp.bfloat16)
    rims_out[1] = side[...].astype(jnp.bfloat16)
    rims_out[2] = state[grid_rows - 2 : grid_rows].reshape(16, width).astype(jnp.bfloat16)
    halos = []
    for index, (row_step, col_step) in enumerate(NEIGHBOURS):
        device = ((above, lat, below)[row_step + 1], lax.rem(lon + n_lon + col_step, n_lon), mem)
        halos.append(send(rims_out.at[row_step + 1], rims_in.at[index],
                          halo_send.at[index], halo_recv.at[index], device))

    whole = sum_over_devices(total, n_lat, n_lon, sum_refs)
    in_sum[...] = whole[0, :, :GROUP].astype(jnp.float32)
    out_sum[:, :GROUP] = whole[0, :, GROUP:].astype(jnp.float32)
    out_sum[:, GROUP:] = whole[1].astype(jnp.float32)

    for copy in halos:
        copy.wait()
    first, last = 8, 8 + grid_cols
    padded[1 : 1 + grid_rows, first:last, :] = state[...]
    for index, (row_step, col_step) in enumerate(NEIGHBOURS):
        rim = rims_in[index].astype(jnp.float32)
        if row_step == 0:
            place = first - 1 if col_step == 1 else last
            start = 0 if col_step == 1 else grid_rows
            for row in range(grid_rows):
                padded[1 + row, place : place + 1, :] = rim[start + row : start + row + 1]
        else:
            line = rim[16 - grid_cols :] * keep_above if row_step == 1 else rim[:grid_cols] * keep_below
            place = 0 if row_step == 1 else 1 + grid_rows
            if col_step == 0:
                padded[place, first:last, :] = line
            elif col_step == 1:
                padded[place, first - 1 : first, :] = line[grid_cols - 1 :]
            else:
                padded[place, last : last + 1, :] = line[:1]
    for group in range(groups):
        lanes = lanes_of(group)
        mixed = padded[1 : 1 + grid_rows, first:last, lanes]
        for index, (row_step, col_step) in enumerate(NEIGHBOURS):
            mixed = mixed + mixing[index : index + 1, lanes] * padded[
                1 + row_step : 1 + row_step + grid_rows, first + col_step : last + col_step, lanes]
        analysis[:, lanes] = mixed.reshape(n_cells, GROUP).astype(jnp.bfloat16)


def per_device(
    measured_inputs,
    target_sector,
    hidden_member_fields,
    analysis_adjoint,
    inner_perceptron_coeffs,
    outer_perceptron_coeffs,
    probe_projector,
    logit_sharpness,
    adjacent_channel_coeffs,
):
    n_lat, n_lon = lax.axis_size("lat"), lax.axis_size("lon")
    n_blocks, block_len, obs_width = measured_inputs.shape
    grid_rows, grid_cols, width = hidden_member_fields.shape[1:]
    hidden_width = inner_perceptron_coeffs.shape[1]
    n_cells = grid_rows * grid_cols
    n_tokens = n_blocks * block_len
    groups = width // GROUP
    sharpness = jnp.repeat(logit_sharpness / math.sqrt(CHANNELS_PER_ATT), CHANNELS_PER_ATT)
    bf16, f32 = jnp.bfloat16, jnp.float32
    vmem, dma = pltpu.VMEM, pltpu.SemaphoreType.DMA
    in_vmem = pl.BlockSpec(memory_space=pltpu.VMEM)
    spread = vmem((n_lon, groups, GROUP, GROUP), bf16)
    scratch = [
        vmem((n_lon, n_cells, width), bf16),
        vmem((n_lon, n_cells, width), bf16),
        vmem((n_lon, 16, width), bf16),
        vmem((n_lon, 16, width), bf16),
        vmem((grid_rows + 2, n_lon * grid_cols, width), f32),
        vmem((width, hidden_width), bf16),
        spread, spread, spread, spread,
        vmem((n_lon, 8, width), f32),
        vmem((n_tokens, width), bf16),
        vmem((n_tokens, hidden_width), bf16),
        vmem((n_tokens, hidden_width), f32),
        vmem((n_blocks, 8, width), f32),
        vmem((n_lon, 4 * n_lon, width), f32),
        vmem((n_lon, 8, width), f32),
        vmem((n_lon, n_cells, width), f32),
        vmem((n_lon, n_cells, width), bf16),
        vmem((n_lon, n_cells, width), bf16),
        vmem((grid_rows, grid_cols, width), f32),
        vmem((16, width), f32),
        vmem((3, 16, width), bf16),
        vmem((8, 16, width), bf16),
        vmem((grid_rows + 2, 24, width), f32),
        vmem((2 * GROUP, 2 * GROUP), f32),
        dma((n_lon,)), dma((n_lon,)), dma((n_lon,)), dma((n_lon,)),
        dma((2, n_lon)), dma((2, n_lon)),
        dma((n_lon,)), dma((n_lon,)), dma((n_lon,)), dma((n_lon,)),
        dma((8,)), dma((8,)),
    ] + sum_scratch(n_lat, n_lon, 2 * GROUP, 2 * GROUP)
    analysis, in_grad, out_grad = pl.pallas_call(
        functools.partial(step_kernel, n_lat, n_lon, n_blocks, grid_rows, grid_cols),
        out_shape=[
            jax.ShapeDtypeStruct((n_cells, width), bf16),
            jax.ShapeDtypeStruct(inner_perceptron_coeffs.shape, f32),
            jax.ShapeDtypeStruct(outer_perceptron_coeffs.shape, f32),
        ],
        in_specs=[pl.BlockSpec(memory_space=pltpu.SMEM)] + [in_vmem] * 8,
        out_specs=[in_vmem] * 3,
        scratch_shapes=scratch,
        compiler_params=pltpu.CompilerParams(
            collective_id=0, has_side_effects=True, vmem_limit_bytes=60 << 20
        ),
        name="assimilation_step",
    )(
        target_sector,
        measured_inputs.reshape(n_tokens, obs_width),
        hidden_member_fields.reshape(n_cells, width),
        analysis_adjoint.reshape(n_cells, width),
        inner_perceptron_coeffs,
        outer_perceptron_coeffs,
        probe_projector,
        sharpness[None, :],
        adjacent_channel_coeffs,
    )
    return (analysis.reshape(hidden_member_fields.shape), in_grad, out_grad)


def solution(mesh):
    in_specs = (
        P(("lat", "lon", "mem"), None, None),
        P(("lat", "lon", "mem")),
        P("mem", "lat", "lon", None),
        P("mem", "lat", "lon", None),
        P(),
        P(),
        P(),
        P(),
        P(),
    )
    out_specs = (P("mem", "lat", "lon", None), P(), P())
    return jax.shard_map(
        per_device, mesh=mesh, in_specs=in_specs, out_specs=out_specs, check_vma=False
    )
```

time: 187 us -> 83.6 us (0.45)
  matrix products: 64.7 us -> 0 us
  Pallas kernels: 23 us -> 76 us
  local copies, waits for them, and re-layouts: 42.9 us -> 6 us
  blocking collectives: 20.7 us -> 0 us
  starting transfers between devices: 16.8 us -> 0 us
  other arithmetic: 16.2 us -> 0.66 us
    dot_general x10 -> x0, matrix products: 64.7 us -> none  [the longest x1 17.7 us: mutual_attention_adjoint(): jnp.einsum('hqk,qhd->khd', logit_grad, query_heads, preferred_element_typ...]
    pallas_call x1, Pallas kernels: 23 us -> 76 us  [per_device(): pl.pallas_call(functools.partial(step_kernel, n_lat, n_lon, n_blocks, gri...]
    unnamed x1 -> x0, blocking collectives: 20.7 us -> none
    another operation x4 -> x1, local copies, waits for them, and re-layouts: 12.5 us -> 0.66 us  [per_device(): sharpness[None, :]]
    ppermute x8 -> x0, starting transfers between devices: 11.6 us -> none  [the longest x4 9.04 us: extended(): lax.ppermute(lax.slice_in_dim(block, 0, width, axis=dim), axis, backward)]
    convert_element_type x1 -> x0, local copies, waits for them, and re-layouts: 8.99 us -> none  [per_device(): obs_feat = jnp.dot(hidden_act, outer_perceptron_coeffs, preferred_element...]
    mul x3 -> x0, other arithmetic: 6.68 us -> none  [the longest x1 5.52 us: silu_slope(): return sigmoid_val * (1.0 + pre_act * (1.0 - sigmoid_val))]
    unnamed x79 -> x3, local copies, waits for them, and re-layouts: 10.8 us -> 5.27 us
  transfers between devices with their start and end apart: 9 -> 0, of which waited for: 0 -> 0; matrix products, arithmetic and copies ran while one was open for 25% -> 0% of each run, Pallas kernels for 12% -> 0%
where the time goes in v2:
time: 83.6 us; the launch traced here: 83.3 us
  Pallas kernels  76 us (91%)
  local copies, waits for them, and re-layouts  6 us (7%)
    pallas_call x1, Pallas kernels, per_device(): pl.pallas_call(functools.partial(step_kernel, n_lat, n_lon, n_blocks, gri...  76 us
    unnamed x3, local copies, waits for them, and re-layouts  5.27 us

profile of v2, /device:TPU:0, one launch (start us, length us, event | category | flops | bytes accessed | tf_op | source)
XLA Modules:
  0.0 83.3 jit_solution(4693879534145708891)
XLA Ops:
  0.6 0.7 broadcast_multiply_fusion
  1.3 0.1 broadcast_in_dim.3
  1.4 0.7 broadcast_in_dim_reshape.3.sharpness
  2.0 76.0 %assimilation_step.1 = (bf16[64,768]{1,0:T(8,128)(2,1)}, f32[256,256]{1,0:T(8,128)}, f32[256,768]{1,0:T(8,128)}) custom-call(s32[16]{0:T(128)} %targets.1, bf16[2048,256]{1,0:T(8,128)(2,1)} %bitcast.4, bf16[64,768]{1,0:T(8,128)(2,1)} %bitcast.6, bf16[64,768]{1,0:T(8,128)(2,1)} %bitcast.7, bf16[256,256]{1,0:T(8,128)(2,1)} %inner.1, bf16[256,768]{1,0:T(8,128)(2,1)} %outer.1, ...), custom_call_target="tpu_custom_call" | custom-call | tf_op jit(solution)/shard_map/assimilation_step/pallas_call | solution.py:486
  78.1 1.5 %copy.15 = bf16[1,8,8,768]{3,2,1,0:T(8,128)(2,1)} copy(bf16[1,8,8,768]{3,2,1,0:T(8,128)(2,1)} %bitcast.5) | data formatting | bytes 196608
  79.6 1.7 %copy.16 = f32[256,256]{1,0:T(8,128)} copy(f32[256,256]{1,0:T(8,128)} %get-tuple-element.13) | data formatting | bytes 524288
  81.3 2.1 %copy.17 = f32[256,768]{1,0:T(8,128)} copy(f32[256,768]{1,0:T(8,128)} %get-tuple-element.14) | data formatting | bytes 1572864

commit v3 on v2

--- a/solution.py
+++ b/solution.py
@@ -145,6 +145,15 @@
     return jnp.where(row_head == col_head, tall, 0.0)
 
 
+def spread_heads_t(cells):
+    n_cells = cells.shape[0]
+    twice = jnp.concatenate([cells, cells], axis=0).T
+    wide = jnp.concatenate([twice] * (GROUP // CHANNELS_PER_ATT // 2), axis=1)
+    row_head = lax.broadcasted_iota(jnp.int32, wide.shape, 0) // CHANNELS_PER_ATT
+    col_head = lax.broadcasted_iota(jnp.int32, wide.shape, 1) // n_cells
+    return jnp.where(row_head == col_head, wide, 0.0)
+
+
 def gather_heads(tall, n_cells):
     col_head = lax.broadcasted_iota(jnp.int32, (n_cells, GROUP), 1) // CHANNELS_PER_ATT
     cells = tall[:n_cells]
@@ -154,12 +163,12 @@
 
 
 def step_kernel(
-    n_lat, n_lon, n_blocks, grid_rows, grid_cols,
-    targets, tokens, latent, cotangent, inner, outer, projector, sharpness, mixing,
-    analysis, in_sum, out_sum,
+    n_lat, n_lon, n_blocks, grid_rows, grid_cols, roomy,
+    targets, head_sharpness, tokens, latent, cotangent, inner, outer, projector, mixing,
+    analysis, sums,
     latents, cots, cots_above, cots_below, band, outer_t,
     query_rows, query_cols, grad_rows, grad_cols, self_rows,
-    features, hidden, slope, block_stats, stats, tile_stats,
+    features, kept, kept_scores, kept_grads, sharpness, hidden, slope, block_stats, stats, tile_stats,
     update, update_out, update_in, state, side, rims_out, rims_in, padded, total,
     lat_send, lat_recv, cot_send, cot_recv, rim_send, rim_recv,
     stat_send, stat_recv, up_send, up_recv, halo_send, halo_recv,
@@ -167,6 +176,7 @@
 ):
     lat, lon, mem = (lax.axis_index(name) for name in ("lat", "lon", "mem"))
     n_cells, width = latent.shape
+    feature_grads = kept if roomy else features
     grads = update
     n_tokens = tokens.shape[0]
     block_len = n_tokens // n_blocks
@@ -203,6 +213,11 @@
         arriving.append(send(cotangent.at[pl.ds(0, 16)], cots_below.at[lon],
                              rim_send.at[1, step], rim_recv.at[1, step],
                              (above, sectors[step], mem)))
+    head = lax.broadcasted_iota(jnp.int32, (1, width), 1) // CHANNELS_PER_ATT
+    row = jnp.zeros((1, width), jnp.float32)
+    for index in range(HEADS):
+        row = jnp.where(head == index, head_sharpness[index], row)
+    sharpness[...] = row / math.sqrt(CHANNELS_PER_ATT)
     latents[lon] = latent[...]
     cots[lon] = cotangent[...]
     outer_t[...] = outer[...].astype(jnp.float32).T.astype(jnp.bfloat16)
@@ -218,7 +233,23 @@
         return carry
 
     lax.fori_loop(0, n_tokens // CHUNK, perceptron, 0)
-    for copy in arriving:
+    for copy in arriving[: n_lon - 1]:
+        copy.wait()
+
+    def prepare_queries(tile, carry):
+        query = dot(latents[tile], projector[...]).astype(jnp.bfloat16).astype(jnp.float32)
+        for group in range(groups):
+            lanes = lanes_of(group)
+            cell_t = spread_heads_t(latents[tile, :, lanes].astype(jnp.float32))
+            spread_t = spread_heads_t(query[:, lanes])
+            query_rows[tile, group] = spread_heads(query[:, lanes]).astype(jnp.bfloat16)
+            query_cols[tile, group] = spread_t.astype(jnp.bfloat16)
+            self_rows[tile, 0:1, lanes] = (
+                jnp.sum(spread_t * cell_t, axis=0, keepdims=True) * sharpness[:, lanes])
+        return carry
+
+    lax.fori_loop(0, n_lon, prepare_queries, 0)
+    for copy in arriving[n_lon - 1 :]:
         copy.wait()
 
     for tile in range(n_lon):
@@ -245,34 +276,29 @@
 
     lax.fori_loop(0, grid_rows, mix_row, 0)
 
-    def prepare(tile, carry):
-        query = dot(latents[tile], projector[...]).astype(jnp.bfloat16).astype(jnp.float32)
+    def prepare_grads(tile, carry):
         for group in range(groups):
             lanes = lanes_of(group)
-            cell_t = spread_heads(latents[tile, :, lanes].astype(jnp.float32)).T
-            spread = spread_heads(query[:, lanes])
-            spread_t = spread.T
-            query_rows[tile, group] = spread.astype(jnp.bfloat16)
-            query_cols[tile, group] = spread_t.astype(jnp.bfloat16)
-            self_rows[tile, 0:1, lanes] = (
-                jnp.sum(spread_t * cell_t, axis=0, keepdims=True) * sharpness[:, lanes])
-            spread = spread_heads(grads[tile, :, lanes])
-            spread_t = spread.T
-            grad_rows[tile, group] = spread.astype(jnp.bfloat16)
+            cell_t = spread_heads_t(latents[tile, :, lanes].astype(jnp.float32))
+            spread_t = spread_heads_t(grads[tile, :, lanes])
+            grad_rows[tile, group] = spread_heads(grads[tile, :, lanes]).astype(jnp.bfloat16)
             grad_cols[tile, group] = spread_t.astype(jnp.bfloat16)
             self_rows[tile, 1:2, lanes] = jnp.sum(spread_t * cell_t, axis=0, keepdims=True)
         return carry
 
-    lax.fori_loop(0, n_lon, prepare, 0)
-
-    def block_sums(block, carry):
-        tile = targets[block]
-        rows = rows_of(block, block_len)
-        for group in range(groups):
+    lax.fori_loop(0, n_lon, prepare_grads, 0)
+
+    def block_sums(pair, carry):
+        for block, group in [(2 * pair + i, j) for i in range(2) for j in range(groups)]:
+            tile = targets[block]
+            rows = rows_of(block, block_len)
             lanes = lanes_of(group)
             feature = features[rows, lanes]
             scores = dot(feature, query_cols[tile, group]) * sharpness[:, lanes]
             weight_grad = dot(feature, grad_cols[tile, group])
+            if roomy:
+                kept_scores[rows, lanes] = scores
+                kept_grads[rows, lanes] = weight_grad
             top = jnp.max(scores, axis=0, keepdims=True)
             exp_terms = jnp.exp(scores - top)
             block_stats[block, 0:1, lanes] = top
@@ -281,7 +307,7 @@
                 exp_terms * weight_grad, axis=0, keepdims=True)
         return carry
 
-    lax.fori_loop(0, n_blocks, block_sums, 0)
+    lax.fori_loop(0, n_blocks // 2, block_sums, 0)
 
     for tile in range(n_lon):
         tops = [jnp.where(targets[block] == tile, block_stats[block, 0:1, :], LOWEST)
@@ -326,21 +352,25 @@
         tile_stats[tile, 2:3, :] = grad_sum * inverse
         tile_stats[tile, 3:4, :] = self_exp * inverse
 
-    def attend(block, carry):
-        tile = targets[block]
-        rows = rows_of(block, block_len)
-        for group in range(groups):
+    def attend(pair, carry):
+        for block, group in [(2 * pair + i, j) for i in range(2) for j in range(groups)]:
+            tile = targets[block]
+            rows = rows_of(block, block_len)
             lanes = lanes_of(group)
             feature = features[rows, lanes]
-            scores = dot(feature, query_cols[tile, group]) * sharpness[:, lanes]
-            weight_grad = dot(feature, grad_cols[tile, group])
+            if roomy:
+                scores = kept_scores[rows, lanes]
+                weight_grad = kept_grads[rows, lanes]
+            else:
+                scores = dot(feature, query_cols[tile, group]) * sharpness[:, lanes]
+                weight_grad = dot(feature, grad_cols[tile, group])
             tile_rows = tile_stats[tile, :, lanes]
             probs = jnp.exp(scores - tile_rows[0:1]) * tile_rows[1:2]
             weights = probs.astype(jnp.bfloat16)
             logit_grad = (
                 probs * (weight_grad - tile_rows[2:3]) * sharpness[:, lanes]
             ).astype(jnp.bfloat16)
-            features[rows, lanes] = (
+            feature_grads[rows, lanes] = (
                 dot(weights, grad_rows[tile, group]) + dot(logit_grad, query_rows[tile, group])
             ).astype(jnp.bfloat16)
             part = gather_heads(dot_rows(weights, feature), n_cells)
@@ -348,7 +378,7 @@
                 update[sector, :, lanes] += jnp.where(tile == sector, part, 0.0)
         return carry
 
-    lax.fori_loop(0, n_blocks, attend, 0)
+    lax.fori_loop(0, n_blocks // 2, attend, 0)
 
     update_out[...] = update[...].astype(jnp.bfloat16)
     arriving = [
@@ -358,7 +388,7 @@
 
     def perceptron_grad(index, carry):
         rows = rows_of(index, CHUNK)
-        feature_grad = features[rows, :]
+        feature_grad = feature_grads[rows, :]
         hidden_grad = (dot(feature_grad, outer_t[...]) * slope[rows, :]).astype(jnp.bfloat16)
         out_grad = dot_rows(hidden[rows, :], feature_grad)
         total[:GROUP, :GROUP] += dot_rows(tokens[rows, :], hidden_grad)
@@ -398,9 +428,7 @@
                           halo_send.at[index], halo_recv.at[index], device))
 
     whole = sum_over_devices(total, n_lat, n_lon, sum_refs)
-    in_sum[...] = whole[0, :, :GROUP].astype(jnp.float32)
-    out_sum[:, :GROUP] = whole[0, :, GROUP:].astype(jnp.float32)
-    out_sum[:, GROUP:] = whole[1].astype(jnp.float32)
+    sums[...] = whole[...]
 
     for copy in halos:
         copy.wait()
@@ -431,6 +459,13 @@
         analysis[:, lanes] = mixed.reshape(n_cells, GROUP).astype(jnp.bfloat16)
 
 
+def finish_kernel(analysis, sums, analysis_out, in_sum, out_sum):
+    analysis_out[...] = analysis[...]
+    in_sum[...] = sums[0, :, :GROUP].astype(jnp.float32)
+    out_sum[:, :GROUP] = sums[0, :, GROUP:].astype(jnp.float32)
+    out_sum[:, GROUP:] = sums[1].astype(jnp.float32)
+
+
 def per_device(
     measured_inputs,
     target_sector,
@@ -449,7 +484,7 @@
     n_cells = grid_rows * grid_cols
     n_tokens = n_blocks * block_len
     groups = width // GROUP
-    sharpness = jnp.repeat(logit_sharpness / math.sqrt(CHANNELS_PER_ATT), CHANNELS_PER_ATT)
+    roomy = n_lon <= 4
     bf16, f32 = jnp.bfloat16, jnp.float32
     vmem, dma = pltpu.VMEM, pltpu.SemaphoreType.DMA
     in_vmem = pl.BlockSpec(memory_space=pltpu.VMEM)
@@ -464,6 +499,10 @@
         spread, spread, spread, spread,
         vmem((n_lon, 8, width), f32),
         vmem((n_tokens, width), bf16),
+        vmem((n_tokens if roomy else 16, width), bf16),
+        vmem((n_tokens if roomy else 8, width), f32),
+        vmem((n_tokens if roomy else 8, width), f32),
+        vmem((1, width), f32),
         vmem((n_tokens, hidden_width), bf16),
         vmem((n_tokens, hidden_width), f32),
         vmem((n_blocks, 8, width), f32),
@@ -483,15 +522,15 @@
         dma((n_lon,)), dma((n_lon,)), dma((n_lon,)), dma((n_lon,)),
         dma((8,)), dma((8,)),
     ] + sum_scratch(n_lat, n_lon, 2 * GROUP, 2 * GROUP)
-    analysis, in_grad, out_grad = pl.pallas_call(
-        functools.partial(step_kernel, n_lat, n_lon, n_blocks, grid_rows, grid_cols),
+    in_smem = pl.BlockSpec(memory_space=pltpu.SMEM)
+    analysis, sums = pl.pallas_call(
+        functools.partial(step_kernel, n_lat, n_lon, n_blocks, grid_rows, grid_cols, roomy),
         out_shape=[
             jax.ShapeDtypeStruct((n_cells, width), bf16),
-            jax.ShapeDtypeStruct(inner_perceptron_coeffs.shape, f32),
-            jax.ShapeDtypeStruct(outer_perceptron_coeffs.shape, f32),
+            jax.ShapeDtypeStruct((2, GROUP, 2 * GROUP), bf16),
         ],
-        in_specs=[pl.BlockSpec(memory_space=pltpu.SMEM)] + [in_vmem] * 8,
-        out_specs=[in_vmem] * 3,
+        in_specs=[in_smem] * 2 + [in_vmem] * 7,
+        out_specs=[in_vmem] * 2,
         scratch_shapes=scratch,
         compiler_params=pltpu.CompilerParams(
             collective_id=0, has_side_effects=True, vmem_limit_bytes=60 << 20
@@ -499,15 +538,27 @@
         name="assimilation_step",
     )(
         target_sector,
+        logit_sharpness,
         measured_inputs.reshape(n_tokens, obs_width),
         hidden_member_fields.reshape(n_cells, width),
         analysis_adjoint.reshape(n_cells, width),
         inner_perceptron_coeffs,
         outer_perceptron_coeffs,
         probe_projector,
-        sharpness[None, :],
         adjacent_channel_coeffs,
     )
+    analysis, in_grad, out_grad = pl.pallas_call(
+        finish_kernel,
+        out_shape=[
+            jax.ShapeDtypeStruct((n_cells, width), bf16),
+            jax.ShapeDtypeStruct(inner_perceptron_coeffs.shape, f32),
+            jax.ShapeDtypeStruct(outer_perceptron_coeffs.shape, f32),
+        ],
+        in_specs=[in_vmem] * 2,
+        out_specs=[in_vmem] * 3,
+        compiler_params=pltpu.CompilerParams(vmem_limit_bytes=16 << 20),
+        name="to_float32",
+    )(analysis, sums)
     return (analysis.reshape(hidden_member_fields.shape), in_grad, out_grad)
 
 

time: 83.6 us -> 67.2 us (0.80)
  Pallas kernels: 76 us -> 64.4 us
  local copies, waits for them, and re-layouts: 6 us -> 1.93 us
    pallas_call x1, Pallas kernels: 76 us -> 63.4 us  [per_device(): pl.pallas_call(functools.partial(step_kernel, n_lat, n_lon, n_blocks, gri...]
    unnamed x3 -> x4, local copies, waits for them, and re-layouts: 5.27 us -> 1.93 us
    pallas_call x0 -> x1, Pallas kernels: none -> 1.05 us  [per_device(): pl.pallas_call(finish_kernel, out_shape=[jax.ShapeDtypeStruct((n_cells, w...]
where the time goes in v3:
time: 67.2 us; the launch traced here: 67 us
  Pallas kernels  64.4 us (96%)
  local copies, waits for them, and re-layouts  1.93 us (3%)
    pallas_call x1, Pallas kernels, per_device(): pl.pallas_call(functools.partial(step_kernel, n_lat, n_lon, n_blocks, gri...  63.4 us
    unnamed x4, local copies, waits for them, and re-layouts  1.93 us

profile of v3, /device:TPU:0, one launch (start us, length us, event | category | flops | bytes accessed | tf_op | source)
XLA Modules:
  0.0 67.0 jit_solution(17332329706034109161)
XLA Ops:
  0.6 63.4 %assimilation_step.1 = (bf16[64,768]{1,0:T(8,128)(2,1)}, bf16[2,256,512]{2,1,0:T(8,128)(2,1)}) custom-call(s32[16]{0:T(128)} %targets.1, f32[12]{0:T(128)} %head_sharpness.1, bf16[2048,256]{1,0:T(8,128)(2,1)} %bitcast.4, bf16[64,768]{1,0:T(8,128)(2,1)} %bitcast.5, bf16[64,768]{1,0:T(8,128)(2,1)} %bitcast.6, bf16[256,256]{1,0:T(8,128)(2,1)} %inner.1, ...), custom_call_target="tpu_custom_call" | custom-call | tf_op jit(solution)/shard_map/assimilation_step/pallas_call | solution.py:526
  64.0 0.0 copy-start
  64.0 1.0 %copy-done = bf16[2,256,512]{2,1,0:T(8,128)(2,1)S(1)} copy-done((bf16[2,256,512]{2,1,0:T(8,128)(2,1)S(1)}, bf16[2,256,512]{2,1,0:T(8,128)(2,1)}, u32[]{:S(2)}) %copy-start) | copy-done | bytes 524312
  65.0 0.0 copy-start.1
  65.1 0.9 %copy-done.1 = bf16[64,768]{1,0:T(8,128)(2,1)S(1)} copy-done((bf16[64,768]{1,0:T(8,128)(2,1)S(1)}, bf16[64,768]{1,0:T(8,128)(2,1)}, u32[]{:S(2)}) %copy-start.1) | copy-done | bytes 98328
  65.9 1.1 %to_float32.1 = (bf16[64,768]{1,0:T(8,128)(2,1)}, f32[256,256]{1,0:T(8,128)}, f32[256,768]{1,0:T(8,128)}) custom-call(bf16[64,768]{1,0:T(8,128)(2,1)S(1)} %copy-done.1, bf16[2,256,512]{2,1,0:T(8,128)(2,1)S(1)} %copy-done), custom_call_target="tpu_custom_call" | custom-call | tf_op jit(solution)/shard_map/to_float32/pallas_call | solution.py:550
Async XLA Ops:
  64.0 1.0 %copy-start = (bf16[2,256,512]{2,1,0:T(8,128)(2,1)S(1)}, bf16[2,256,512]{2,1,0:T(8,128)(2,1)}, u32[]{:S(2)}) copy-start(bf16[2,256,512]{2,1,0:T(8,128)(2,1)} %get-tuple-element.9.sums) | copy-start | bytes 1572868
  65.0 0.9 %copy-start.1 = (bf16[64,768]{1,0:T(8,128)(2,1)S(1)}, bf16[64,768]{1,0:T(8,128)(2,1)}, u32[]{:S(2)}) copy-start(bf16[64,768]{1,0:T(8,128)(2,1)} %get-tuple-element.8.analysis) | copy-start | bytes 294916

commit v4 on v3

--- a/solution.py
+++ b/solution.py
@@ -18,99 +18,74 @@
 NEIGHBOURS = ((-1, -1), (-1, 0), (-1, 1), (0, -1), (0, 1), (1, -1), (1, 0), (1, 1))
 
 MESH = pl.DeviceIdType.MESH
-
-
-def sum_scratch(n_lat, n_lon, rows, width):
-    half = rows // 2
-    part = half // n_lon
+PIECE = 128
+
+
+def sum_scratch(n_lat, n_lon, pieces, rows):
+    peers = 2 * n_lon
+    part = rows // peers
+    by_peer = pltpu.VMEM((pieces, peers, part, PIECE), jnp.bfloat16)
     return [
-        pltpu.VMEM((rows, width), jnp.bfloat16),
-        pltpu.VMEM((half, width), jnp.bfloat16),
-        pltpu.VMEM((half, width), jnp.float32),
-        pltpu.VMEM((n_lon, part, width), jnp.bfloat16),
-        pltpu.VMEM((n_lon, part, width), jnp.bfloat16),
-        pltpu.VMEM((n_lat, part, width), jnp.bfloat16),
-        pltpu.VMEM((2, half, width), jnp.bfloat16),
-        pltpu.SemaphoreType.DMA((2,)),
-        pltpu.SemaphoreType.DMA((2,)),
-        pltpu.SemaphoreType.DMA((2, n_lon)),
-        pltpu.SemaphoreType.DMA((2, n_lon)),
-        pltpu.SemaphoreType.DMA((n_lat,)),
-        pltpu.SemaphoreType.DMA((n_lat,)),
+        by_peer, by_peer,
+        pltpu.VMEM((pieces, n_lat, part, PIECE), jnp.bfloat16),
+        by_peer,
+        pltpu.SemaphoreType.DMA((pieces, 2, peers)),
+        pltpu.SemaphoreType.DMA((pieces, 2, peers)),
+        pltpu.SemaphoreType.DMA((pieces, n_lat)),
+        pltpu.SemaphoreType.DMA((pieces, n_lat)),
     ]
 
 
-def sum_over_devices(total, n_lat, n_lon, scratch):
-    (rounded, from_core, half_sum, to_lon, from_lon, by_lat, whole,
-     core_send, core_recv, lon_send, lon_recv, lat_send, lat_recv) = scratch
+def sum_piece(piece, total, n_lat, n_lon, scratch):
+    rounded, arrived, by_lat, whole, peer_send, peer_recv, lat_send, lat_recv = scratch
     lat, lon, mem = (lax.axis_index(name) for name in ("lat", "lon", "mem"))
-    other = 1 - mem
-    rows = total.shape[0]
-    half = rows // 2
-    part = half // n_lon
-
-    rounded[...] = total[...].astype(jnp.bfloat16)
-    away = pl.ds(pl.multiple_of(other * half, half), half)
-    copy = pltpu.make_async_remote_copy(
-        src_ref=rounded.at[away], dst_ref=from_core,
-        send_sem=core_send.at[0], recv_sem=core_recv.at[0],
-        device_id=(lat, lon, other), device_id_type=MESH)
-    copy.start()
-    copy.wait()
-    mine = pl.ds(pl.multiple_of(mem * half, half), half)
-    half_sum[...] = total[mine, :] + from_core[...].astype(jnp.float32)
-
-    to_lon[...] = half_sum[...].astype(jnp.bfloat16).reshape(to_lon.shape)
+    peers = 2 * n_lon
+    part = total.shape[1] // peers
+    me = 2 * lon + mem
+
+    rounded[piece] = total[piece].astype(jnp.bfloat16).reshape(rounded.shape[1:])
     copies = []
-    for step in range(1, n_lon):
-        peer = lax.rem(lon + step, n_lon)
-        copy = pltpu.make_async_remote_copy(
-            src_ref=to_lon.at[peer], dst_ref=from_lon.at[step],
-            send_sem=lon_send.at[0, step], recv_sem=lon_recv.at[0, step],
-            device_id=(lat, peer, mem), device_id_type=MESH)
-        copy.start()
-        copies.append(copy)
-    part_sum = half_sum[pl.ds(pl.multiple_of(lon * part, part), part), :]
+    for step in range(1, peers):
+        peer = lax.rem(me + step, peers)
+        copies.append(pltpu.make_async_remote_copy(
+            src_ref=rounded.at[piece, peer], dst_ref=arrived.at[piece, step],
+            send_sem=peer_send.at[piece, 0, step], recv_sem=peer_recv.at[piece, 0, step],
+            device_id=(lat, lax.div(peer, 2), lax.rem(peer, 2)), device_id_type=MESH))
+        copies[-1].start()
+    yield
+    part_sum = total[piece, pl.ds(pl.multiple_of(me * part, part), part), :]
     for step, copy in enumerate(copies, 1):
         copy.wait()
-        part_sum = part_sum + from_lon[step].astype(jnp.float32)
-
-    by_lat[lat] = part_sum.astype(jnp.bfloat16)
+        part_sum = part_sum + arrived[piece, step].astype(jnp.float32)
+
+    by_lat[piece, lat] = part_sum.astype(jnp.bfloat16)
     copies = []
     for step in range(1, n_lat):
-        peer = lax.rem(lat + step, n_lat)
-        copy = pltpu.make_async_remote_copy(
-            src_ref=by_lat.at[lat], dst_ref=by_lat.at[lat],
-            send_sem=lat_send.at[step], recv_sem=lat_recv.at[step],
-            device_id=(peer, lon, mem), device_id_type=MESH)
-        copy.start()
-        copies.append(copy)
+        copies.append(pltpu.make_async_remote_copy(
+            src_ref=by_lat.at[piece, lat], dst_ref=by_lat.at[piece, lat],
+            send_sem=lat_send.at[piece, step], recv_sem=lat_recv.at[piece, step],
+            device_id=(lax.rem(lat + step, n_lat), lon, mem), device_id_type=MESH))
+        copies[-1].start()
+    yield
     for copy in copies:
         copy.wait()
-    band_sum = by_lat[0].astype(jnp.float32)
+    band_sum = by_lat[piece, 0].astype(jnp.float32)
     for index in range(1, n_lat):
-        band_sum = band_sum + by_lat[index].astype(jnp.float32)
-
-    own = pl.ds(pl.multiple_of(lon * part, part), part)
-    whole[mem, own, :] = band_sum.astype(jnp.bfloat16)
+        band_sum = band_sum + by_lat[piece, index].astype(jnp.float32)
+
+    whole[piece, me] = band_sum.astype(jnp.bfloat16)
     copies = []
-    for step in range(1, n_lon):
-        peer = lax.rem(lon + step, n_lon)
-        copy = pltpu.make_async_remote_copy(
-            src_ref=whole.at[mem, own], dst_ref=whole.at[mem, own],
-            send_sem=lon_send.at[1, step], recv_sem=lon_recv.at[1, step],
-            device_id=(lat, peer, mem), device_id_type=MESH)
-        copy.start()
-        copies.append(copy)
+    for step in range(1, peers):
+        peer = lax.rem(me + step, peers)
+        copies.append(pltpu.make_async_remote_copy(
+            src_ref=whole.at[piece, me], dst_ref=whole.at[piece, me],
+            send_sem=peer_send.at[piece, 1, step], recv_sem=peer_recv.at[piece, 1, step],
+            device_id=(lat, lax.div(peer, 2), lax.rem(peer, 2)), device_id_type=MESH))
+        copies[-1].start()
+    yield
     for copy in copies:
         copy.wait()
-    copy = pltpu.make_async_remote_copy(
-        src_ref=whole.at[mem], dst_ref=whole.at[mem],
-        send_sem=core_send.at[1], recv_sem=core_recv.at[1],
-        device_id=(lat, lon, other), device_id_type=MESH)
-    copy.start()
-    copy.wait()
-    return whole
+    yield
 
 
 def greet(partners):
@@ -168,7 +143,7 @@
     analysis, sums,
     latents, cots, cots_above, cots_below, band, outer_t,
     query_rows, query_cols, grad_rows, grad_cols, self_rows,
-    features, kept, kept_scores, kept_grads, sharpness, hidden, slope, block_stats, stats, tile_stats,
+    features, kept, kept_scores, kept_grads, sharpness, hidden_t, tokens_t, slope, block_stats, stats, tile_stats,
     update, update_out, update_in, state, side, rims_out, rims_in, padded, total,
     lat_send, lat_recv, cot_send, cot_recv, rim_send, rim_recv,
     stat_send, stat_recv, up_send, up_recv, halo_send, halo_recv,
@@ -186,8 +161,8 @@
     keep_below = jnp.where(lat < n_lat - 1, 1.0, 0.0)
     sectors = [lax.rem(lon + step, n_lon) for step in range(n_lon)]
 
-    partners = [(lat, lon, 1 - mem)]
-    partners += [(lat, sector, mem) for sector in sectors[1:]]
+    partners = [(lat, sector, mem) for sector in sectors[1:]]
+    partners += [(lat, sector, 1 - mem) for sector in sectors]
     partners += [(row, sector, mem) for row in (above, below) for sector in sectors]
     partners += [(lax.rem(lat + step, n_lat), lon, mem) for step in range(2, n_lat - 1)]
     greet(partners)
@@ -228,7 +203,8 @@
         sigmoid_val = jax.nn.sigmoid(pre_act)
         slope[rows, :] = sigmoid_val * (1.0 + pre_act * (1.0 - sigmoid_val))
         hidden_act = (pre_act * sigmoid_val).astype(jnp.bfloat16)
-        hidden[rows, :] = hidden_act
+        hidden_t[:, rows] = hidden_act.T
+        tokens_t[:, rows] = tokens[rows, :].T
         features[rows, :] = dot(hidden_act, outer[...]).astype(jnp.bfloat16)
         return carry
 
@@ -352,51 +328,81 @@
         tile_stats[tile, 2:3, :] = grad_sum * inverse
         tile_stats[tile, 3:4, :] = self_exp * inverse
 
-    def attend(pair, carry):
-        for block, group in [(2 * pair + i, j) for i in range(2) for j in range(groups)]:
-            tile = targets[block]
-            rows = rows_of(block, block_len)
-            lanes = lanes_of(group)
-            feature = features[rows, lanes]
-            if roomy:
-                scores = kept_scores[rows, lanes]
-                weight_grad = kept_grads[rows, lanes]
-            else:
-                scores = dot(feature, query_cols[tile, group]) * sharpness[:, lanes]
-                weight_grad = dot(feature, grad_cols[tile, group])
-            tile_rows = tile_stats[tile, :, lanes]
-            probs = jnp.exp(scores - tile_rows[0:1]) * tile_rows[1:2]
-            weights = probs.astype(jnp.bfloat16)
-            logit_grad = (
-                probs * (weight_grad - tile_rows[2:3]) * sharpness[:, lanes]
-            ).astype(jnp.bfloat16)
-            feature_grads[rows, lanes] = (
-                dot(weights, grad_rows[tile, group]) + dot(logit_grad, query_rows[tile, group])
-            ).astype(jnp.bfloat16)
-            part = gather_heads(dot_rows(weights, feature), n_cells)
-            for sector in range(n_lon):
-                update[sector, :, lanes] += jnp.where(tile == sector, part, 0.0)
+    def attend(group, first, last):
+        lanes = lanes_of(group)
+
+        def four_blocks(index, carry):
+            for block in [4 * index + i for i in range(4)]:
+                tile = targets[block]
+                rows = rows_of(block, block_len)
+                feature = features[rows, lanes]
+                if roomy:
+                    scores = kept_scores[rows, lanes]
+                    weight_grad = kept_grads[rows, lanes]
+                else:
+                    scores = dot(feature, query_cols[tile, group]) * sharpness[:, lanes]
+                    weight_grad = dot(feature, grad_cols[tile, group])
+                tile_rows = tile_stats[tile, :, lanes]
+                probs = jnp.exp(scores - tile_rows[0:1]) * tile_rows[1:2]
+                weights = probs.astype(jnp.bfloat16)
+                logit_grad = (
+                    probs * (weight_grad - tile_rows[2:3]) * sharpness[:, lanes]
+                ).astype(jnp.bfloat16)
+                feature_grads[rows, lanes] = (
+                    dot(weights, grad_rows[tile, group])
+                    + dot(logit_grad, query_rows[tile, group])
+                ).astype(jnp.bfloat16)
+                part = gather_heads(dot_rows(weights, feature), n_cells)
+                for sector in range(n_lon):
+                    update[sector, :, lanes] += jnp.where(tile == sector, part, 0.0)
+            return carry
+
+        lax.fori_loop(first * n_blocks // 8, last * n_blocks // 8, four_blocks, 0)
+
+    def out_grad(group):
+        product = dot(hidden_t[...], feature_grads[:, lanes_of(group)])
+        total[1 + group, :GROUP, :] = product[:, :PIECE]
+        total[1 + group, GROUP:, :] = product[:, PIECE:]
+
+    def perceptron_grad(index, carry):
+        rows = rows_of(index, CHUNK)
+        feature_grad = feature_grads[rows, :]
+        hidden_grad = (dot(feature_grad, outer_t[...]) * slope[rows, :]).astype(jnp.bfloat16)
+        product = dot(tokens_t[:, rows], hidden_grad)
+        total[0, :GROUP, :] += product[:, :PIECE]
+        total[0, GROUP:, :] += product[:, PIECE:]
         return carry
 
-    lax.fori_loop(0, n_blocks // 2, attend, 0)
-
+    sums_of = [sum_piece(piece, total, n_lat, n_lon, sum_refs) for piece in range(1 + groups)]
+
+    def advance(*pieces):
+        for piece in pieces:
+            next(sums_of[piece])
+
+    attend(0, 0, 2)
+    out_grad(0)
+    advance(1)
+    attend(1, 0, 1)
+    advance(1)
+    attend(1, 1, 2)
+    out_grad(1)
+    advance(1, 2)
+    attend(2, 0, 1)
+    advance(1, 2)
+    attend(2, 1, 2)
     update_out[...] = update[...].astype(jnp.bfloat16)
     arriving = [
         send(update_out.at[sectors[step]], update_in.at[step], up_send.at[step], up_recv.at[step],
              (lat, sectors[step], mem))
         for step in range(1, n_lon)]
 
-    def perceptron_grad(index, carry):
-        rows = rows_of(index, CHUNK)
-        feature_grad = feature_grads[rows, :]
-        hidden_grad = (dot(feature_grad, outer_t[...]) * slope[rows, :]).astype(jnp.bfloat16)
-        out_grad = dot_rows(hidden[rows, :], feature_grad)
-        total[:GROUP, :GROUP] += dot_rows(tokens[rows, :], hidden_grad)
-        total[:GROUP, GROUP:] += out_grad[:, :GROUP]
-        total[GROUP:, :] += out_grad[:, GROUP:]
-        return carry
-
-    lax.fori_loop(0, n_tokens // CHUNK, perceptron_grad, 0)
+    out_grad(2)
+    advance(2, 3)
+    chunks = n_tokens // CHUNK
+    lax.fori_loop(0, chunks // 2, perceptron_grad, 0)
+    advance(2, 3)
+    lax.fori_loop(chunks // 2, chunks, perceptron_grad, 0)
+    advance(0, 3)
 
     for copy in arriving:
         copy.wait()
@@ -427,9 +433,7 @@
         halos.append(send(rims_out.at[row_step + 1], rims_in.at[index],
                           halo_send.at[index], halo_recv.at[index], device))
 
-    whole = sum_over_devices(total, n_lat, n_lon, sum_refs)
-    sums[...] = whole[...]
-
+    advance(0, 3)
     for copy in halos:
         copy.wait()
     first, last = 8, 8 + grid_cols
@@ -450,6 +454,7 @@
                 padded[place, first - 1 : first, :] = line[grid_cols - 1 :]
             else:
                 padded[place, last : last + 1, :] = line[:1]
+    advance(0)
     for group in range(groups):
         lanes = lanes_of(group)
         mixed = padded[1 : 1 + grid_rows, first:last, lanes]
@@ -457,13 +462,18 @@
             mixed = mixed + mixing[index : index + 1, lanes] * padded[
                 1 + row_step : 1 + row_step + grid_rows, first + col_step : last + col_step, lanes]
         analysis[:, lanes] = mixed.reshape(n_cells, GROUP).astype(jnp.bfloat16)
+    advance(0)
+    sums[...] = sum_refs[3][...].reshape(sums.shape)
 
 
 def finish_kernel(analysis, sums, analysis_out, in_sum, out_sum):
     analysis_out[...] = analysis[...]
-    in_sum[...] = sums[0, :, :GROUP].astype(jnp.float32)
-    out_sum[:, :GROUP] = sums[0, :, GROUP:].astype(jnp.float32)
-    out_sum[:, GROUP:] = sums[1].astype(jnp.float32)
+    in_sum[:, :PIECE] = sums[0, :GROUP].astype(jnp.float32)
+    in_sum[:, PIECE:] = sums[0, GROUP:].astype(jnp.float32)
+    for group in range(out_sum.shape[1] // GROUP):
+        middle = group * GROUP + PIECE
+        out_sum[:, middle - PIECE : middle] = sums[1 + group, :GROUP].astype(jnp.float32)
+        out_sum[:, middle : middle + PIECE] = sums[1 + group, GROUP:].astype(jnp.float32)
 
 
 def per_device(
@@ -503,7 +513,8 @@
         vmem((n_tokens if roomy else 8, width), f32),
         vmem((n_tokens if roomy else 8, width), f32),
         vmem((1, width), f32),
-        vmem((n_tokens, hidden_width), bf16),
+        vmem((hidden_width, n_tokens), bf16),
+        vmem((obs_width, n_tokens), bf16),
         vmem((n_tokens, hidden_width), f32),
         vmem((n_blocks, 8, width), f32),
         vmem((n_lon, 4 * n_lon, width), f32),
@@ -516,18 +527,18 @@
         vmem((3, 16, width), bf16),
         vmem((8, 16, width), bf16),
         vmem((grid_rows + 2, 24, width), f32),
-        vmem((2 * GROUP, 2 * GROUP), f32),
+        vmem((1 + groups, 2 * GROUP, PIECE), f32),
         dma((n_lon,)), dma((n_lon,)), dma((n_lon,)), dma((n_lon,)),
         dma((2, n_lon)), dma((2, n_lon)),
         dma((n_lon,)), dma((n_lon,)), dma((n_lon,)), dma((n_lon,)),
         dma((8,)), dma((8,)),
-    ] + sum_scratch(n_lat, n_lon, 2 * GROUP, 2 * GROUP)
+    ] + sum_scratch(n_lat, n_lon, 1 + groups, 2 * GROUP)
     in_smem = pl.BlockSpec(memory_space=pltpu.SMEM)
     analysis, sums = pl.pallas_call(
         functools.partial(step_kernel, n_lat, n_lon, n_blocks, grid_rows, grid_cols, roomy),
         out_shape=[
             jax.ShapeDtypeStruct((n_cells, width), bf16),
-            jax.ShapeDtypeStruct((2, GROUP, 2 * GROUP), bf16),
+            jax.ShapeDtypeStruct((1 + groups, 2 * GROUP, PIECE), bf16),
         ],
         in_specs=[in_smem] * 2 + [in_vmem] * 7,
         out_specs=[in_vmem] * 2,

time: 67.2 us -> 74.8 us (1.11)
  Pallas kernels: 64.4 us -> 72 us
    pallas_call x1, Pallas kernels: 63.4 us -> 71 us  [per_device(): pl.pallas_call(functools.partial(step_kernel, n_lat, n_lon, n_blocks, gri...]
where the time goes in v4:
time: 74.8 us; the launch traced here: 74.6 us
  Pallas kernels  72 us (96%)
  local copies, waits for them, and re-layouts  1.93 us (3%)
    pallas_call x1, Pallas kernels, per_device(): pl.pallas_call(functools.partial(step_kernel, n_lat, n_lon, n_blocks, gri...  71 us
    unnamed x4, local copies, waits for them, and re-layouts  1.93 us

profile of v4, /device:TPU:0, one launch (start us, length us, event | category | flops | bytes accessed | tf_op | source)
XLA Modules:
  0.0 74.6 jit_solution(11475140087880597235)
XLA Ops:
  0.6 71.0 %assimilation_step.1 = (bf16[64,768]{1,0:T(8,128)(2,1)}, bf16[4,512,128]{2,1,0:T(8,128)(2,1)}) custom-call(s32[16]{0:T(128)} %targets.1, f32[12]{0:T(128)} %head_sharpness.1, bf16[2048,256]{1,0:T(8,128)(2,1)} %bitcast.4, bf16[64,768]{1,0:T(8,128)(2,1)} %bitcast.5, bf16[64,768]{1,0:T(8,128)(2,1)} %bitcast.6, bf16[256,256]{1,0:T(8,128)(2,1)} %inner.1, ...), custom_call_target="tpu_custom_call" | custom-call | tf_op jit(solution)/shard_map/assimilation_step/pallas_call | solution.py:537
  71.6 0.0 copy-start
  71.6 1.0 %copy-done = bf16[4,512,128]{2,1,0:T(8,128)(2,1)S(1)} copy-done((bf16[4,512,128]{2,1,0:T(8,128)(2,1)S(1)}, bf16[4,512,128]{2,1,0:T(8,128)(2,1)}, u32[]{:S(2)}) %copy-start) | copy-done | bytes 524312
  72.6 0.0 copy-start.1
  72.6 0.9 %copy-done.1 = bf16[64,768]{1,0:T(8,128)(2,1)S(1)} copy-done((bf16[64,768]{1,0:T(8,128)(2,1)S(1)}, bf16[64,768]{1,0:T(8,128)(2,1)}, u32[]{:S(2)}) %copy-start.1) | copy-done | bytes 98328
  73.5 1.1 %to_float32.1 = (bf16[64,768]{1,0:T(8,128)(2,1)}, f32[256,256]{1,0:T(8,128)}, f32[256,768]{1,0:T(8,128)}) custom-call(bf16[64,768]{1,0:T(8,128)(2,1)S(1)} %copy-done.1, bf16[4,512,128]{2,1,0:T(8,128)(2,1)S(1)} %copy-done), custom_call_target="tpu_custom_call" | custom-call | tf_op jit(solution)/shard_map/to_float32/pallas_call | solution.py:561
Async XLA Ops:
  71.6 1.0 %copy-start = (bf16[4,512,128]{2,1,0:T(8,128)(2,1)S(1)}, bf16[4,512,128]{2,1,0:T(8,128)(2,1)}, u32[]{:S(2)}) copy-start(bf16[4,512,128]{2,1,0:T(8,128)(2,1)} %get-tuple-element.9.sums) | copy-start | bytes 1572868
  72.6 0.9 %copy-start.1 = (bf16[64,768]{1,0:T(8,128)(2,1)S(1)}, bf16[64,768]{1,0:T(8,128)(2,1)}, u32[]{:S(2)}) copy-start(bf16[64,768]{1,0:T(8,128)(2,1)} %get-tuple-element.8.analysis) | copy-start | bytes 294916

commit v5 on v3

--- a/solution.py
+++ b/solution.py
@@ -40,7 +40,7 @@
     ]
 
 
-def sum_over_devices(total, n_lat, n_lon, scratch):
+def sum_stages(total, n_lat, n_lon, scratch):
     (rounded, from_core, half_sum, to_lon, from_lon, by_lat, whole,
      core_send, core_recv, lon_send, lon_recv, lat_send, lat_recv) = scratch
     lat, lon, mem = (lax.axis_index(name) for name in ("lat", "lon", "mem"))
@@ -56,6 +56,7 @@
         send_sem=core_send.at[0], recv_sem=core_recv.at[0],
         device_id=(lat, lon, other), device_id_type=MESH)
     copy.start()
+    yield
     copy.wait()
     mine = pl.ds(pl.multiple_of(mem * half, half), half)
     half_sum[...] = total[mine, :] + from_core[...].astype(jnp.float32)
@@ -70,6 +71,7 @@
             device_id=(lat, peer, mem), device_id_type=MESH)
         copy.start()
         copies.append(copy)
+    yield
     part_sum = half_sum[pl.ds(pl.multiple_of(lon * part, part), part), :]
     for step, copy in enumerate(copies, 1):
         copy.wait()
@@ -85,6 +87,7 @@
             device_id=(peer, lon, mem), device_id_type=MESH)
         copy.start()
         copies.append(copy)
+    yield
     for copy in copies:
         copy.wait()
     band_sum = by_lat[0].astype(jnp.float32)
@@ -102,6 +105,7 @@
             device_id=(lat, peer, mem), device_id_type=MESH)
         copy.start()
         copies.append(copy)
+    yield
     for copy in copies:
         copy.wait()
     copy = pltpu.make_async_remote_copy(
@@ -109,8 +113,9 @@
         send_sem=core_send.at[1], recv_sem=core_recv.at[1],
         device_id=(lat, lon, other), device_id_type=MESH)
     copy.start()
+    yield
     copy.wait()
-    return whole
+    yield
 
 
 def greet(partners):
@@ -352,8 +357,8 @@
         tile_stats[tile, 2:3, :] = grad_sum * inverse
         tile_stats[tile, 3:4, :] = self_exp * inverse
 
-    def attend(pair, carry):
-        for block, group in [(2 * pair + i, j) for i in range(2) for j in range(groups)]:
+    def attend(chosen, count, step, carry):
+        for block, group in [(count * step + i, j) for i in range(count) for j in chosen]:
             tile = targets[block]
             rows = rows_of(block, block_len)
             lanes = lanes_of(group)
@@ -378,8 +383,28 @@
                 update[sector, :, lanes] += jnp.where(tile == sector, part, 0.0)
         return carry
 
-    lax.fori_loop(0, n_blocks // 2, attend, 0)
-
+    def attend_loop(chosen, first, last):
+        count = 4 // len(chosen)
+        body = functools.partial(attend, chosen, count)
+        lax.fori_loop(first * n_blocks // (8 * count), last * n_blocks // (8 * count), body, 0)
+
+    def out_grad(index, carry):
+        rows = rows_of(index, CHUNK)
+        product = dot_rows(hidden[rows, :], feature_grads[rows, : 2 * GROUP])
+        total[0, :GROUP, :] += product[:, :GROUP]
+        total[0, GROUP:, :] += product[:, GROUP:]
+        return carry
+
+    first_sum, last_sum = [
+        sum_stages(total.at[index], n_lat, n_lon, sum_refs[index :: 2]) for index in range(2)]
+    chunks = n_tokens // CHUNK
+    attend_loop((0, 1), 0, 8)
+    lax.fori_loop(0, chunks, out_grad, 0)
+    next(first_sum)
+    attend_loop((2,), 0, 4)
+    next(first_sum)
+    attend_loop((2,), 4, 8)
+    next(first_sum)
     update_out[...] = update[...].astype(jnp.bfloat16)
     arriving = [
         send(update_out.at[sectors[step]], update_in.at[step], up_send.at[step], up_recv.at[step],
@@ -390,13 +415,15 @@
         rows = rows_of(index, CHUNK)
         feature_grad = feature_grads[rows, :]
         hidden_grad = (dot(feature_grad, outer_t[...]) * slope[rows, :]).astype(jnp.bfloat16)
-        out_grad = dot_rows(hidden[rows, :], feature_grad)
-        total[:GROUP, :GROUP] += dot_rows(tokens[rows, :], hidden_grad)
-        total[:GROUP, GROUP:] += out_grad[:, :GROUP]
-        total[GROUP:, :] += out_grad[:, GROUP:]
-        return carry
-
-    lax.fori_loop(0, n_tokens // CHUNK, perceptron_grad, 0)
+        total[1, :GROUP, :] += dot_rows(tokens[rows, :], hidden_grad)
+        total[1, GROUP:, :] += dot_rows(hidden[rows, :], feature_grad[:, 2 * GROUP :])
+        return carry
+
+    lax.fori_loop(0, chunks // 2, perceptron_grad, 0)
+    next(first_sum)
+    lax.fori_loop(chunks // 2, chunks, perceptron_grad, 0)
+    next(last_sum)
+    next(first_sum)
 
     for copy in arriving:
         copy.wait()
@@ -427,9 +454,9 @@
         halos.append(send(rims_out.at[row_step + 1], rims_in.at[index],
                           halo_send.at[index], halo_recv.at[index], device))
 
-    whole = sum_over_devices(total, n_lat, n_lon, sum_refs)
-    sums[...] = whole[...]
-
+    next(last_sum)
+    next(first_sum)
+    next(last_sum)
     for copy in halos:
         copy.wait()
     first, last = 8, 8 + grid_cols
@@ -450,6 +477,7 @@
                 padded[place, first - 1 : first, :] = line[grid_cols - 1 :]
             else:
                 padded[place, last : last + 1, :] = line[:1]
+    next(last_sum)
     for group in range(groups):
         lanes = lanes_of(group)
         mixed = padded[1 : 1 + grid_rows, first:last, lanes]
@@ -457,13 +485,17 @@
             mixed = mixed + mixing[index : index + 1, lanes] * padded[
                 1 + row_step : 1 + row_step + grid_rows, first + col_step : last + col_step, lanes]
         analysis[:, lanes] = mixed.reshape(n_cells, GROUP).astype(jnp.bfloat16)
+    next(last_sum)
+    next(last_sum)
+    sums[0] = sum_refs[12][...]
+    sums[1] = sum_refs[13][...]
 
 
 def finish_kernel(analysis, sums, analysis_out, in_sum, out_sum):
     analysis_out[...] = analysis[...]
-    in_sum[...] = sums[0, :, :GROUP].astype(jnp.float32)
-    out_sum[:, :GROUP] = sums[0, :, GROUP:].astype(jnp.float32)
-    out_sum[:, GROUP:] = sums[1].astype(jnp.float32)
+    in_sum[...] = sums[1, 0].astype(jnp.float32)
+    for group, (index, part) in enumerate(((0, 0), (0, 1), (1, 1))):
+        out_sum[:, lanes_of(group)] = sums[index, part].astype(jnp.float32)
 
 
 def per_device(
@@ -516,18 +548,20 @@
         vmem((3, 16, width), bf16),
         vmem((8, 16, width), bf16),
         vmem((grid_rows + 2, 24, width), f32),
-        vmem((2 * GROUP, 2 * GROUP), f32),
+        vmem((2, 2 * GROUP, GROUP), f32),
         dma((n_lon,)), dma((n_lon,)), dma((n_lon,)), dma((n_lon,)),
         dma((2, n_lon)), dma((2, n_lon)),
         dma((n_lon,)), dma((n_lon,)), dma((n_lon,)), dma((n_lon,)),
         dma((8,)), dma((8,)),
-    ] + sum_scratch(n_lat, n_lon, 2 * GROUP, 2 * GROUP)
+    ] + [
+        ref for ref in sum_scratch(n_lat, n_lon, 2 * GROUP, GROUP) for _ in range(2)
+    ]
     in_smem = pl.BlockSpec(memory_space=pltpu.SMEM)
     analysis, sums = pl.pallas_call(
         functools.partial(step_kernel, n_lat, n_lon, n_blocks, grid_rows, grid_cols, roomy),
         out_shape=[
             jax.ShapeDtypeStruct((n_cells, width), bf16),
-            jax.ShapeDtypeStruct((2, GROUP, 2 * GROUP), bf16),
+            jax.ShapeDtypeStruct((2, 2, GROUP, GROUP), bf16),
         ],
         in_specs=[in_smem] * 2 + [in_vmem] * 7,
         out_specs=[in_vmem] * 2,

time: 67.2 us -> 68.6 us (1.021)
  Pallas kernels: 64.4 us -> 65.7 us
    pallas_call x1, Pallas kernels: 63.4 us -> 64.7 us  [per_device(): pl.pallas_call(functools.partial(step_kernel, n_lat, n_lon, n_blocks, gri...]
where the time goes in v5:
time: 68.6 us; the launch traced here: 68.3 us
  Pallas kernels  65.7 us (96%)
  local copies, waits for them, and re-layouts  1.93 us (3%)
    pallas_call x1, Pallas kernels, per_device(): pl.pallas_call(functools.partial(step_kernel, n_lat, n_lon, n_blocks, gri...  64.7 us
    unnamed x4, local copies, waits for them, and re-layouts  1.93 us

profile of v5, /device:TPU:0, one launch (start us, length us, event | category | flops | bytes accessed | tf_op | source)
XLA Modules:
  0.0 68.3 jit_solution(12167481518489604134)
XLA Ops:
  0.6 64.7 %assimilation_step.1 = (bf16[64,768]{1,0:T(8,128)(2,1)}, bf16[2,2,256,256]{3,2,1,0:T(8,128)(2,1)}) custom-call(s32[16]{0:T(128)} %targets.1, f32[12]{0:T(128)} %head_sharpness.1, bf16[2048,256]{1,0:T(8,128)(2,1)} %bitcast.4, bf16[64,768]{1,0:T(8,128)(2,1)} %bitcast.5, bf16[64,768]{1,0:T(8,128)(2,1)} %bitcast.6, bf16[256,256]{1,0:T(8,128)(2,1)} %inner.1, ...), custom_call_target="tpu_custom_call" | custom-call | tf_op jit(solution)/shard_map/assimilation_step/pallas_call | solution.py:560
  65.3 0.0 copy-start
  65.3 1.0 %copy-done = bf16[2,2,256,256]{3,2,1,0:T(8,128)(2,1)S(1)} copy-done((bf16[2,2,256,256]{3,2,1,0:T(8,128)(2,1)S(1)}, bf16[2,2,256,256]{3,2,1,0:T(8,128)(2,1)}, u32[]{:S(2)}) %copy-start) | copy-done | bytes 524312
  66.4 0.0 copy-start.1
  66.4 0.9 %copy-done.1 = bf16[64,768]{1,0:T(8,128)(2,1)S(1)} copy-done((bf16[64,768]{1,0:T(8,128)(2,1)S(1)}, bf16[64,768]{1,0:T(8,128)(2,1)}, u32[]{:S(2)}) %copy-start.1) | copy-done | bytes 98328
  67.3 1.1 %to_float32.1 = (bf16[64,768]{1,0:T(8,128)(2,1)}, f32[256,256]{1,0:T(8,128)}, f32[256,768]{1,0:T(8,128)}) custom-call(bf16[64,768]{1,0:T(8,128)(2,1)S(1)} %copy-done.1, bf16[2,2,256,256]{3,2,1,0:T(8,128)(2,1)S(1)} %copy-done), custom_call_target="tpu_custom_call" | custom-call | tf_op jit(solution)/shard_map/to_float32/pallas_call | solution.py:584
Async XLA Ops:
  65.3 1.0 %copy-start = (bf16[2,2,256,256]{3,2,1,0:T(8,128)(2,1)S(1)}, bf16[2,2,256,256]{3,2,1,0:T(8,128)(2,1)}, u32[]{:S(2)}) copy-start(bf16[2,2,256,256]{3,2,1,0:T(8,128)(2,1)} %get-tuple-element.9.sums) | copy-start | bytes 1572868
  66.4 0.9 %copy-start.1 = (bf16[64,768]{1,0:T(8,128)(2,1)S(1)}, bf16[64,768]{1,0:T(8,128)(2,1)}, u32[]{:S(2)}) copy-start(bf16[64,768]{1,0:T(8,128)(2,1)} %get-tuple-element.8.analysis) | copy-start | bytes 294916

commit v6 on v3

--- a/solution.py
+++ b/solution.py
@@ -288,8 +288,8 @@
 
     lax.fori_loop(0, n_lon, prepare_grads, 0)
 
-    def block_sums(pair, carry):
-        for block, group in [(2 * pair + i, j) for i in range(2) for j in range(groups)]:
+    def block_sums(quad, carry):
+        for block, group in [(4 * quad + i, j) for i in range(4) for j in range(groups)]:
             tile = targets[block]
             rows = rows_of(block, block_len)
             lanes = lanes_of(group)
@@ -307,7 +307,7 @@
                 exp_terms * weight_grad, axis=0, keepdims=True)
         return carry
 
-    lax.fori_loop(0, n_blocks // 2, block_sums, 0)
+    lax.fori_loop(0, n_blocks // 4, block_sums, 0)
 
     for tile in range(n_lon):
         tops = [jnp.where(targets[block] == tile, block_stats[block, 0:1, :], LOWEST)
@@ -352,8 +352,8 @@
         tile_stats[tile, 2:3, :] = grad_sum * inverse
         tile_stats[tile, 3:4, :] = self_exp * inverse
 
-    def attend(pair, carry):
-        for block, group in [(2 * pair + i, j) for i in range(2) for j in range(groups)]:
+    def attend(quad, carry):
+        for block, group in [(4 * quad + i, j) for i in range(4) for j in range(groups)]:
             tile = targets[block]
             rows = rows_of(block, block_len)
             lanes = lanes_of(group)
@@ -378,7 +378,7 @@
                 update[sector, :, lanes] += jnp.where(tile == sector, part, 0.0)
         return carry
 
-    lax.fori_loop(0, n_blocks // 2, attend, 0)
+    lax.fori_loop(0, n_blocks // 4, attend, 0)
 
     update_out[...] = update[...].astype(jnp.bfloat16)
     arriving = [

time: 67.2 us -> 65.7 us (0.978)
  Pallas kernels: 64.4 us -> 62.9 us
    pallas_call x1, Pallas kernels: 63.4 us -> 61.9 us  [per_device(): pl.pallas_call(functools.partial(step_kernel, n_lat, n_lon, n_blocks, gri...]
where the time goes in v6:
time: 65.7 us; the launch traced here: 65.5 us
  Pallas kernels  62.9 us (96%)
  local copies, waits for them, and re-layouts  1.93 us (3%)
    pallas_call x1, Pallas kernels, per_device(): pl.pallas_call(functools.partial(step_kernel, n_lat, n_lon, n_blocks, gri...  61.9 us
    unnamed x4, local copies, waits for them, and re-layouts  1.93 us

profile of v6, /device:TPU:0, one launch (start us, length us, event | category | flops | bytes accessed | tf_op | source)
XLA Modules:
  0.0 65.5 jit_solution(8421764211764173227)
XLA Ops:
  0.6 61.9 %assimilation_step.1 = (bf16[64,768]{1,0:T(8,128)(2,1)}, bf16[2,256,512]{2,1,0:T(8,128)(2,1)}) custom-call(s32[16]{0:T(128)} %targets.1, f32[12]{0:T(128)} %head_sharpness.1, bf16[2048,256]{1,0:T(8,128)(2,1)} %bitcast.4, bf16[64,768]{1,0:T(8,128)(2,1)} %bitcast.5, bf16[64,768]{1,0:T(8,128)(2,1)} %bitcast.6, bf16[256,256]{1,0:T(8,128)(2,1)} %inner.1, ...), custom_call_target="tpu_custom_call" | custom-call | tf_op jit(solution)/shard_map/assimilation_step/pallas_call | solution.py:526
  62.5 0.0 copy-start
  62.5 1.0 %copy-done = bf16[2,256,512]{2,1,0:T(8,128)(2,1)S(1)} copy-done((bf16[2,256,512]{2,1,0:T(8,128)(2,1)S(1)}, bf16[2,256,512]{2,1,0:T(8,128)(2,1)}, u32[]{:S(2)}) %copy-start) | copy-done | bytes 524312
  63.6 0.0 copy-start.1
  63.6 0.9 %copy-done.1 = bf16[64,768]{1,0:T(8,128)(2,1)S(1)} copy-done((bf16[64,768]{1,0:T(8,128)(2,1)S(1)}, bf16[64,768]{1,0:T(8,128)(2,1)}, u32[]{:S(2)}) %copy-start.1) | copy-done | bytes 98328
  64.4 1.1 %to_float32.1 = (bf16[64,768]{1,0:T(8,128)(2,1)}, f32[256,256]{1,0:T(8,128)}, f32[256,768]{1,0:T(8,128)}) custom-call(bf16[64,768]{1,0:T(8,128)(2,1)S(1)} %copy-done.1, bf16[2,256,512]{2,1,0:T(8,128)(2,1)S(1)} %copy-done), custom_call_target="tpu_custom_call" | custom-call | tf_op jit(solution)/shard_map/to_float32/pallas_call | solution.py:550
Async XLA Ops:
  62.5 1.0 %copy-start = (bf16[2,256,512]{2,1,0:T(8,128)(2,1)S(1)}, bf16[2,256,512]{2,1,0:T(8,128)(2,1)}, u32[]{:S(2)}) copy-start(bf16[2,256,512]{2,1,0:T(8,128)(2,1)} %get-tuple-element.9.sums) | copy-start | bytes 1572868
  63.6 0.9 %copy-start.1 = (bf16[64,768]{1,0:T(8,128)(2,1)S(1)}, bf16[64,768]{1,0:T(8,128)(2,1)}, u32[]{:S(2)}) copy-start(bf16[64,768]{1,0:T(8,128)(2,1)} %get-tuple-element.8.analysis) | copy-start | bytes 294916
